TPU v7x, 512 devices: a whole 4x4x16 slice. The times are simulated.
512 devices in a mesh: corpus: 32 (over y, x, core), conv: 16 (over z).
Axes of the slice: x: 4, y: 4, z: 16, core: 2. Of those that a mesh axis runs over, the one named last changes fastest.
Arguments:
- queries: bfloat16 [65536, 2048], P(('corpus', 'conv')), may hold values from -128 to 128
- cotangent: bfloat16 [65536, 2048], P(('corpus', 'conv')), may hold values from -6 to 6
- corpus_of: int32 [65536, 1], P(('corpus', 'conv')), may hold values from 0 to 31, as said below
- cartridge: bfloat16 [32, 2048, 1024], P('corpus', 'conv'), may hold values from -6 to 6
Outputs:
- attended: bfloat16 [65536, 2048], P(('corpus', 'conv'))
- cartridge_grad: float32 [32, 2048, 1024], P('corpus', 'conv')
Inputs may be any that keep to these rules, and one draw needn't show every extreme that they name: `corpus_of`: every block of 128 rows holds the same labels: token t belongs to conversation t % 128, and each conversation to one corpus. Every corpus has 1 to 5 conversations, and some corpus exactly 5.
All inputs are finite; a program needn't handle non-finite values.
Results may differ from a plain program's by a relative error of at most 0.03.
Values may be sent and summed in bfloat16 or wider, within the bound.
No kernel may reach another device: no remote copies, remote signals or barrier semaphores. Data moves between devices by JAX's collectives and lax.ppermute only.
A program may use at most 128 MiB of HBM per device.

v0:
```python
import jax
import jax.numpy as jnp
from jax import lax
from jax.sharding import PartitionSpec as P

HEAD_DIM = 128


def place_rows(values, position, slot_count):
    return jnp.zeros((slot_count, values.shape[1]), values.dtype).at[position].set(values)


def local(queries, cotangent, corpus_of, cartridge):
    tokens = queries.shape[0]
    owners = lax.axis_size("corpus")
    capacity = 5 * tokens // (4 * owners)
    slot_count = owners * capacity
    target = corpus_of[:, 0]
    member = (target[:, None] == jnp.arange(owners, dtype=jnp.int32)[None, :]).astype(jnp.int32)
    earlier = jnp.cumsum(member, axis=0) - member
    position = target * capacity + jnp.sum(earlier * member, axis=1)
    sent_queries = lax.all_to_all(
        place_rows(queries, position, slot_count), "corpus", split_axis=0, concat_axis=0, tiled=True
    )
    gathered = lax.all_gather(cartridge, "conv", axis=1, tiled=True)[0]
    kv_width = gathered.shape[1] // 2
    kv_heads = kv_width // HEAD_DIM
    per_group = queries.shape[1] // kv_width
    score_scale = HEAD_DIM ** (-0.5)
    query_heads = sent_queries.reshape(slot_count, kv_heads, per_group, HEAD_DIM)
    prob_list = []
    max_list = []
    sum_list = []
    outputs = []
    for head in range(kv_heads):
        key_head = gathered[:, head * HEAD_DIM : (head + 1) * HEAD_DIM]
        value_head = gathered[:, kv_width + head * HEAD_DIM : kv_width + (head + 1) * HEAD_DIM]
        scores = (
            jnp.einsum(
                "sgd,rd->sgr", query_heads[:, head], key_head, preferred_element_type=jnp.float32
            )
            * score_scale
        )
        row_max = jnp.max(scores, axis=2, keepdims=True)
        weights = jnp.exp(scores - row_max)
        row_sum = jnp.sum(weights, axis=2, keepdims=True)
        probs = (weights / row_sum).astype(jnp.bfloat16)
        outputs.append(
            jnp.einsum("sgr,rd->sgd", probs, value_head, preferred_element_type=jnp.float32)
        )
        prob_list.append(probs)
        max_list.append(row_max)
        sum_list.append(row_sum)
    head_outs = jnp.stack(outputs, axis=1)
    replies = lax.all_to_all(
        head_outs.reshape(slot_count, -1).astype(jnp.bfloat16),
        "corpus",
        split_axis=0,
        concat_axis=0,
        tiled=True,
    )
    attended = replies[position]
    sent_grads = lax.all_to_all(
        place_rows(cotangent, position, slot_count),
        "corpus",
        split_axis=0,
        concat_axis=0,
        tiled=True,
    )
    grad_heads = sent_grads.reshape(slot_count, kv_heads, per_group, HEAD_DIM)
    row_delta = jnp.sum(grad_heads.astype(jnp.float32) * head_outs, axis=3, keepdims=True)
    key_grads = []
    value_grads = []
    for head in range(kv_heads):
        value_slice = gathered[:, kv_width + head * HEAD_DIM : kv_width + (head + 1) * HEAD_DIM]
        probs = prob_list[head]
        value_grads.append(
            jnp.einsum(
                "sgr,sgd->rd", probs, grad_heads[:, head], preferred_element_type=jnp.float32
            )
        )
        prob_grad = jnp.einsum(
            "sgd,rd->sgr", grad_heads[:, head], value_slice, preferred_element_type=jnp.float32
        )
        score_grad = (probs.astype(jnp.float32) * (prob_grad - row_delta[:, head])).astype(
            jnp.bfloat16
        )
        key_grads.append(
            jnp.einsum(
                "sgr,sgd->rd", score_grad, query_heads[:, head], preferred_element_type=jnp.float32
            )
            * score_scale
        )
    cartridge_grad = lax.psum_scatter(
        jnp.concatenate(key_grads + value_grads, axis=1).astype(jnp.bfloat16),
        "conv",
        scatter_dimension=0,
        tiled=True,
    ).astype(jnp.float32)
    return (attended, cartridge_grad[None])


def solution(mesh):
    return jax.shard_map(
        local,
        mesh=mesh,
        in_specs=(
            P(("corpus", "conv"), None),
            P(("corpus", "conv"), None),
            P(("corpus", "conv"), None),
            P("corpus", "conv", None),
        ),
        out_specs=(P(("corpus", "conv"), None), P("corpus", "conv", None)),
        check_vma=False,
    )
```

profile of v0, /device:TPU:6, one launch (start us, length us, event | category | flops | bytes accessed | tf_op | source)
XLA Modules:
  0.0 254.9 jit_solution(8983613614619891543)
XLA Ops:
  13.7 9.5 %all-to-all-start.2 = ((bf16[32,5,2048]{2,1,0:T(8,128)(2,1)}), bf16[32,5,2048]{2,1,0:T(8,128)(2,1)S(1)}, u32[]{:S(2)}, u32[]{:S(2)}) async-start(bf16[32,5,2048]{2,1,0:T(8,128)(2,1)} %all_to_all.22), calls=%async_computation.2 | async-start | bytes 2097152 | tf_op jit(solution)/shard_map/all_to_all | solution.py:63
  26.5 11.4 %all-to-all-done.2 = bf16[32,5,2048]{2,1,0:T(8,128)(2,1)S(1)} async-done(((bf16[32,5,2048]{2,1,0:T(8,128)(2,1)}), bf16[32,5,2048]{2,1,0:T(8,128)(2,1)S(1)}, u32[]{:S(2)}, u32[]{:S(2)}) %all-to-all-start.2) | async-done | bytes 655392 | tf_op jit(solution)/shard_map/all_to_all | solution.py:63
  37.9 6.6 %all-to-all-start = ((bf16[32,5,2048]{2,1,0:T(8,128)(2,1)}), bf16[32,5,2048]{2,1,0:T(8,128)(2,1)S(1)}, u32[]{:S(2)}, u32[]{:S(2)}) async-start(bf16[32,5,2048]{2,1,0:T(8,128)(2,1)} %all_to_all.18), calls=%async_computation | async-start | bytes 2097152 | tf_op jit(solution)/shard_map/all_to_all | solution.py:22
  46.3 12.8 %all-to-all-done = bf16[32,5,2048]{2,1,0:T(8,128)(2,1)S(1)} async-done(((bf16[32,5,2048]{2,1,0:T(8,128)(2,1)}), bf16[32,5,2048]{2,1,0:T(8,128)(2,1)S(1)}, u32[]{:S(2)}, u32[]{:S(2)}) %all-to-all-start) | async-done | bytes 655392 | tf_op jit(solution)/shard_map/all_to_all | solution.py:22
  60.8 32.4 %all-gather.2.cloned.1.call-done = bf16[1,2048,1024]{2,1,0:T(8,128)(2,1)} async-done(((bf16[1,128,1024]{2,1,0:T(8,128)(2,1)}), bf16[1,2048,1024]{2,1,0:T(8,128)(2,1)}) %all-gather.2.cloned.1.call-update) | async-done | bytes 4194320 | tf_op jit(solution)/shard_map/all_gather | solution.py:25
  93.2 5.2 %fusion.67 = (f32[160,4]{0,1:T(4,128)S(1)}, f32[160,4,2048]{2,0,1:T(8,128)}) fusion(bf16[2048,1024]{1,0:T(8,128)(2,1)} %bitcast.230, bf16[160,1,4,128]{3,2,1,0:T(4,128)(2,1)S(1)} %get-tuple-element.8), kind=kOutput, calls=%fused_computation.114 | convolution fusion | flops 339478528 | bytes 5933568 | tf_op jit(solution)/shard_map/sub | solution.py:45
  98.4 3.2 %divide_convert_fusion.3 = bf16[160,4,2048]{2,0,1:T(8,128)(2,1)S(1)} fusion(f32[160,4,2048]{2,0,1:T(8,128)} %get-tuple-element.23, f32[160,4]{0,1:T(4,128)S(1)} %get-tuple-element.22), kind=kLoop, calls=%fused_computation.17 | loop fusion | flops 2621440 | bytes 7866880 | tf_op jit(solution)/shard_map/convert_element_type | solution.py:47
  101.6 2.6 %convolution_bitcast_fusion.11 = f32[160,1,4,128]{3,0,2,1:T(8,128)} fusion(bf16[160,4,2048]{2,0,1:T(8,128)(2,1)S(1)} %divide_convert_fusion.3, bf16[2048,1024]{1,0:T(8,128)(2,1)} %bitcast.231), kind=kOutput, calls=%fused_computation.64 | convolution fusion | flops 335544320 | bytes 3473408 | tf_op jit(solution)/shard_map/sgr,rd->sgd/dot_general | solution.py:49
  104.3 5.2 %fusion.65 = (f32[160,4]{0,1:T(4,128)S(1)}, f32[160,4,2048]{2,0,1:T(8,128)}) fusion(bf16[2048,1024]{1,0:T(8,128)(2,1)} %bitcast.232, bf16[160,1,4,128]{3,2,1,0:T(4,128)(2,1)} %get-tuple-element.9), kind=kOutput, calls=%fused_computation.112 | convolution fusion | flops 339478528 | bytes 5933568 | tf_op jit(solution)/shard_map/sub | solution.py:45
  109.5 3.2 %divide_convert_fusion.1 = bf16[160,4,2048]{2,0,1:T(8,128)(2,1)S(1)} fusion(f32[160,4,2048]{2,0,1:T(8,128)} %get-tuple-element.19, f32[160,4]{0,1:T(4,128)S(1)} %get-tuple-element.18), kind=kLoop, calls=%fused_computation.13 | loop fusion | flops 2621440 | bytes 7866880 | tf_op jit(solution)/shard_map/convert_element_type | solution.py:47
  114.2 2.6 %convolution_bitcast_fusion.9 = f32[160,1,4,128]{3,0,2,1:T(8,128)} fusion(bf16[160,4,2048]{2,0,1:T(8,128)(2,1)S(1)} %divide_convert_fusion.1, bf16[2048,1024]{1,0:T(8,128)(2,1)} %bitcast.233), kind=kOutput, calls=%fused_computation.62 | convolution fusion | flops 335544320 | bytes 3473408 | tf_op jit(solution)/shard_map/sgr,rd->sgd/dot_general | solution.py:49
  116.9 5.2 %fusion.66 = (f32[160,4]{0,1:T(4,128)S(1)}, f32[160,4,2048]{2,0,1:T(8,128)}) fusion(bf16[2048,1024]{1,0:T(8,128)(2,1)} %bitcast.234, bf16[160,1,4,128]{3,2,1,0:T(4,128)(2,1)} %get-tuple-element.10), kind=kOutput, calls=%fused_computation.113 | convolution fusion | flops 339478528 | bytes 5933568 | tf_op jit(solution)/shard_map/sub | solution.py:45
  122.1 3.2 %divide_convert_fusion.2 = bf16[160,4,2048]{2,0,1:T(8,128)(2,1)S(1)} fusion(f32[160,4,2048]{2,0,1:T(8,128)} %get-tuple-element.21, f32[160,4]{0,1:T(4,128)S(1)} %get-tuple-element.20), kind=kLoop, calls=%fused_computation.15 | loop fusion | flops 2621440 | bytes 7866880 | tf_op jit(solution)/shard_map/convert_element_type | solution.py:47
  126.9 2.6 %convolution_bitcast_fusion.10 = f32[160,1,4,128]{3,0,2,1:T(8,128)} fusion(bf16[160,4,2048]{2,0,1:T(8,128)(2,1)S(1)} %divide_convert_fusion.2, bf16[2048,1024]{1,0:T(8,128)(2,1)} %bitcast.235), kind=kOutput, calls=%fused_computation.63 | convolution fusion | flops 335544320 | bytes 3473408 | tf_op jit(solution)/shard_map/sgr,rd->sgd/dot_general | solution.py:49
  129.5 5.4 %fusion.64 = (f32[160,4]{0,1:T(4,128)S(1)}, f32[160,4,2048]{2,0,1:T(8,128)}) fusion(bf16[2048,1024]{1,0:T(8,128)(2,1)} %bitcast.236, bf16[160,1,4,128]{3,2,1,0:T(4,128)(2,1)S(1)} %get-tuple-element.11), kind=kOutput, calls=%fused_computation.111 | convolution fusion | flops 339478528 | bytes 5933568 | tf_op jit(solution)/shard_map/sub | solution.py:45
  134.9 3.3 %divide_convert_fusion = bf16[160,4,2048]{2,0,1:T(8,128)(2,1)S(1)} fusion(f32[160,4,2048]{2,0,1:T(8,128)} %get-tuple-element.17, f32[160,4]{0,1:T(4,128)S(1)} %get-tuple-element.16), kind=kLoop, calls=%fused_computation.11 | loop fusion | flops 2621440 | bytes 7866880 | tf_op jit(solution)/shard_map/convert_element_type | solution.py:47
  141.3 3.3 %fusion.31 = bf16[2048,1024]{0,1:T(8,128)(2,1)} fusion(bf16[160,4,2048]{2,0,1:T(8,128)(2,1)S(1)} %divide_convert_fusion.3, f32[160,4]{0,1:T(4,128)S(1)} %get-tuple-element.15, bf16[2048,1024]{1,0:T(8,128)(2,1)} %bitcast.238, bf16[160,4,4,128]{3,0,2,1:T(8,128)(2,1)} %copy.23, bf16[160,1,4,128]{3,2,1,0:T(4,128)(2,1)} %copy-done.15), kind=kOutput, calls=%fused_computation.50 | convolution fusion | flops 676855808 | bytes 4000256 | tf_op jit(solution)/shard_map/sgr,sgd->rd/dot_general | solution.py:89
  144.6 4.0 %fusion.30 = bf16[2048,1024]{0,1:T(8,128)(2,1)} fusion(bf16[2048,1024]{0,1:T(8,128)(2,1)} %fusion.31, bf16[160,4,2048]{2,0,1:T(8,128)(2,1)} %copy-done.2, f32[160,4]{0,1:T(4,128)S(1)} %get-tuple-element.14, bf16[2048,1024]{1,0:T(8,128)(2,1)} %bitcast.239, bf16[160,4,4,128]{3,0,2,1:T(8,128)(2,1)S(1)} %copy-done.14, ...), kind=kOutput, calls=%fused_computation.49 | convolution fusion | flops 676855808 | bytes 4001792 | tf_op jit(solution)/shard_map/sgr,sgd->rd/dot_general | solution.py:89
  148.6 4.0 %fusion.29 = bf16[2048,1024]{0,1:T(8,128)(2,1)} fusion(bf16[2048,1024]{0,1:T(8,128)(2,1)} %fusion.30, bf16[160,4,2048]{2,0,1:T(8,128)(2,1)} %copy-done, f32[160,4]{0,1:T(4,128)S(1)} %get-tuple-element.13, bf16[2048,1024]{1,0:T(8,128)(2,1)} %bitcast.240, bf16[160,4,4,128]{3,0,2,1:T(8,128)(2,1)S(1)} %copy-done.14, bf16[160,1,4,128]{3,2,1,0:T(4,128)(2,1)} %get-tuple-element.9), kind=kOutput, calls=%fused_computation.48 | convolution fusion | flops 676855808 | bytes 4001792 | tf_op jit(solution)/shard_map/sgr,sgd->rd/dot_general | solution.py:89
  152.6 4.1 %fusion.28 = bf16[2048,1024]{0,1:T(8,128)(2,1)} fusion(bf16[2048,1024]{0,1:T(8,128)(2,1)} %fusion.29, bf16[160,4,2048]{2,0,1:T(8,128)(2,1)} %copy-done.4, f32[160,4]{0,1:T(4,128)S(1)} %get-tuple-element.12, bf16[2048,1024]{1,0:T(8,128)(2,1)} %bitcast.241, bf16[160,4,4,128]{3,0,2,1:T(8,128)(2,1)S(1)} %copy-done.14, ...), kind=kOutput, calls=%fused_computation.47 | convolution fusion | flops 676855808 | bytes 4001792 | tf_op jit(solution)/shard_map/sgr,sgd->rd/dot_general | solution.py:89
  163.0 6.4 %copy.29 = bf16[2048,1024]{1,0:T(8,128)(2,1)} copy(bf16[2048,1024]{0,1:T(8,128)(2,1)} %fusion.39) | data formatting | bytes 8388608
  172.4 7.4 %all-to-all-start.1 = ((bf16[32,5,2048]{2,1,0:T(8,128)(2,1)}), bf16[32,5,2048]{2,1,0:T(8,128)(2,1)S(1)}, u32[]{:S(2)}, u32[]{:S(2)}) async-start(bf16[32,5,2048]{2,1,0:T(8,128)(2,1)} %convert_element_type.57), calls=%async_computation.1 | async-start | bytes 2097152 | tf_op jit(solution)/shard_map/all_to_all | solution.py:55
  179.8 14.6 %all-to-all-done.1 = bf16[32,5,2048]{2,1,0:T(8,128)(2,1)S(1)} async-done(((bf16[32,5,2048]{2,1,0:T(8,128)(2,1)}), bf16[32,5,2048]{2,1,0:T(8,128)(2,1)S(1)}, u32[]{:S(2)}, u32[]{:S(2)}) %all-to-all-start.1) | async-done | bytes 655392 | tf_op jit(solution)/shard_map/all_to_all | solution.py:55
  196.4 49.5 %reduce-scatter.4.cloned.1.call-done = bf16[128,1024]{1,0:T(8,128)(2,1)} async-done(((bf16[2048,1024]{1,0:T(8,128)(2,1)}), bf16[128,1024]{1,0:T(8,128)(2,1)}) %reduce-scatter.4.cloned.1.call-update) | async-done | bytes 262160
  (64 shorter events, 32.8 us)
Async XLA Ops:
  7.2 86.0 %all-gather.2.cloned.1.call-start = ((), (), s32[]{:S(2)}) async-start(), calls=%async_computation.4 | async-start | bytes 4456448 | tf_op jit(solution)/shard_map/all_gather | solution.py:25
  13.7 24.2 %all-to-all-start.2 = ((bf16[32,5,2048]{2,1,0:T(8,128)(2,1)}), bf16[32,5,2048]{2,1,0:T(8,128)(2,1)S(1)}, u32[]{:S(2)}, u32[]{:S(2)}) async-start(bf16[32,5,2048]{2,1,0:T(8,128)(2,1)} %all_to_all.22), calls=%async_computation.2 | async-start | bytes 2097152 | tf_op jit(solution)/shard_map/all_to_all | solution.py:63
  37.9 21.3 %all-to-all-start = ((bf16[32,5,2048]{2,1,0:T(8,128)(2,1)}), bf16[32,5,2048]{2,1,0:T(8,128)(2,1)S(1)}, u32[]{:S(2)}, u32[]{:S(2)}) async-start(bf16[32,5,2048]{2,1,0:T(8,128)(2,1)} %all_to_all.18), calls=%async_computation | async-start | bytes 2097152 | tf_op jit(solution)/shard_map/all_to_all | solution.py:22
  44.4 201.5 %reduce-scatter.4.cloned.1.call-start = ((), (), s32[]{:S(2)}) async-start(), calls=%async_computation.5 | async-start | bytes 4456448
  60.8 37.6 %copy-start.15 = (bf16[160,1,4,128]{3,2,1,0:T(4,128)(2,1)}, bf16[160,1,4,128]{3,2,1,0:T(4,128)(2,1)S(1)}, u32[]{:S(2)}) copy-start(bf16[160,1,4,128]{3,2,1,0:T(4,128)(2,1)S(1)} %get-tuple-element.8) | copy-start | bytes 491524
  112.8 1.5 copy-start
  125.4 1.5 copy-start.2
  134.9 5.7 %copy-start.6 = (f32[160,1,4,128]{3,0,2,1:T(8,128)S(1)}, f32[160,1,4,128]{3,0,2,1:T(8,128)}, u32[]{:S(2)}) copy-start(f32[160,1,4,128]{3,0,2,1:T(8,128)} %convolution_bitcast_fusion.11) | copy-start | bytes 983044
  134.9 5.7 %copy-start.8 = (f32[160,1,4,128]{3,0,2,1:T(8,128)S(1)}, f32[160,1,4,128]{3,0,2,1:T(8,128)}, u32[]{:S(2)}) copy-start(f32[160,1,4,128]{3,0,2,1:T(8,128)} %convolution_bitcast_fusion.9) | copy-start | bytes 983044
  134.9 5.7 %copy-start.10 = (f32[160,1,4,128]{3,0,2,1:T(8,128)S(1)}, f32[160,1,4,128]{3,0,2,1:T(8,128)}, u32[]{:S(2)}) copy-start(f32[160,1,4,128]{3,0,2,1:T(8,128)} %convolution_bitcast_fusion.10) | copy-start | bytes 983044
  138.3 3.0 %copy-start.4 = (bf16[160,4,2048]{2,0,1:T(8,128)(2,1)}, bf16[160,4,2048]{2,0,1:T(8,128)(2,1)S(1)}, u32[]{:S(2)}) copy-start(bf16[160,4,2048]{2,0,1:T(8,128)(2,1)S(1)} %divide_convert_fusion) | copy-start | bytes 7864324
  140.6 0.7 copy-start.12
  141.3 3.4 %copy-start.14 = (bf16[160,4,4,128]{3,0,2,1:T(8,128)(2,1)S(1)}, bf16[160,4,4,128]{3,0,2,1:T(8,128)(2,1)}, u32[]{:S(2)}) copy-start(bf16[160,4,4,128]{3,0,2,1:T(8,128)(2,1)} %copy.23) | copy-start | bytes 1966084
  156.7 1.9 copy-start.3
  156.7 3.4 %copy-start.1 = (bf16[160,4,2048]{2,0,1:T(8,128)(2,1)S(1)}, bf16[160,4,2048]{2,0,1:T(8,128)(2,1)}, u32[]{:S(2)}) copy-start(bf16[160,4,2048]{2,0,1:T(8,128)(2,1)} %copy-done) | copy-start | bytes 7864324
  158.6 2.9 %copy-start.5 = (bf16[160,4,2048]{2,0,1:T(8,128)(2,1)S(1)}, bf16[160,4,2048]{2,0,1:T(8,128)(2,1)}, u32[]{:S(2)}) copy-start(bf16[160,4,2048]{2,0,1:T(8,128)(2,1)} %copy-done.4) | copy-start | bytes 7864324
  169.4 1.0 copy-start.7
  169.4 1.1 copy-start.9
  169.4 1.2 copy-start.11
  169.4 1.3 copy-start.13
  172.4 22.0 %all-to-all-start.1 = ((bf16[32,5,2048]{2,1,0:T(8,128)(2,1)}), bf16[32,5,2048]{2,1,0:T(8,128)(2,1)S(1)}, u32[]{:S(2)}, u32[]{:S(2)}) async-start(bf16[32,5,2048]{2,1,0:T(8,128)(2,1)} %convert_element_type.57), calls=%async_computation.1 | async-start | bytes 2097152 | tf_op jit(solution)/shard_map/all_to_all | solution.py:55
Sparse Core Ops, SparseCore 0:
  10.1 83.0 all-gather.1
  169.5 76.3 reduce-scatter.3
where the time goes:
time: 256 us; the launch traced here: 255 us
  waiting for transfers between devices  121 us (47%)
  matrix products  52.4 us (20%)
  local copies, waits for them, and re-layouts  26.9 us (11%)
  starting transfers between devices  23.7 us (9%)
  other arithmetic  16.3 us (6%)
  between operations  14.3 us (6%)
    unnamed x3, waiting for transfers between devices  50.2 us
    all_gather x1, waiting for transfers between devices, local(): gathered = lax.all_gather(cartridge, 'conv', axis=1, tiled=True)[0]  32.4 us
    sub x4, matrix products, local(): weights = jnp.exp(scores - row_max)  21.1 us
    dot_general x4, matrix products, local(): jnp.einsum('sgr,sgd->rd', score_grad, query_heads[:, head], preferred_ele...  15.3 us
    all_to_all x1, waiting for transfers between devices, local(): lax.all_to_all(head_outs.reshape(slot_count, -1).astype(jnp.bfloat16), 'c...  14.6 us
    unnamed x35, local copies, waits for them, and re-layouts  13.3 us
    convert_element_type x4, other arithmetic, local(): probs = (weights / row_sum).astype(jnp.bfloat16)  13.1 us
    all_to_all x1, waiting for transfers between devices, local(): lax.all_to_all(place_rows(queries, position, slot_count), 'corpus', split...  12.8 us
  transfers between devices with their start and end apart: 5, of which 5 were waited for; matrix products, arithmetic and copies ran while one was open for 5% of the time, Pallas kernels for 0%

commit v1 on v0

v1 whole, which is shorter than its diff:
```python
import functools

import jax
import jax.numpy as jnp
from jax import lax
from jax.experimental import pallas as pl
from jax.experimental.pallas import tpu as pltpu
from jax.sharding import PartitionSpec as P

HEAD_DIM = 128
KV_HEADS = 4
GROUP = 4
CAP = 5
OWNERS = 32
RING = 16
ROWS = 2048
SHARD = ROWS // RING
TOK = 128
SLAB = OWNERS * 8
QUERIES = OWNERS * CAP * GROUP
BLOCK = 512
SCALE = HEAD_DIM ** -0.5
EXP2_SCALE = SCALE * 1.4426950408889634
RECV_STEP = 5
DONE_STEP = 7
VMEM_LIMIT = 56 * 1024 * 1024

f32 = jnp.float32
bf16 = jnp.bfloat16


def dot(a, b):
    return jnp.dot(a, b, preferred_element_type=f32)


def iota(shape, dim):
    return lax.broadcasted_iota(jnp.int32, shape, dim)


def one_hot(mask):
    return jnp.where(mask, 1.0, 0.0).astype(bf16)


def bases(owner, rank):
    out = []
    for first in (0, 2):
        here = (rank >= first) & (rank < first + 2)
        out.append(jnp.where(here, owner * 8 + (rank - first) * 4, -64))
    out.append(jnp.where(rank == 4, owner * 8, -64))
    return out


def pack_kernel(row_ref, col_ref, q_ref, c_ref, out_ref):
    row = row_ref[...]
    same = jnp.broadcast_to(col_ref[...], (TOK, TOK)) == jnp.broadcast_to(row, (TOK, TOK))
    before = iota((TOK, TOK), 0) < iota((TOK, TOK), 1)
    rank = jnp.sum(jnp.where(same & before, 1, 0), axis=0, keepdims=True)
    base = bases(row, rank)
    slab_row = iota((SLAB, TOK), 0)

    def place(first, count):
        wide = jnp.broadcast_to(first, (SLAB, TOK))
        return jnp.concatenate([one_hot(slab_row == wide + j) for j in range(count)], axis=1)

    def head(ref, h):
        return ref[:, h * HEAD_DIM:(h + 1) * HEAD_DIM]

    full = jnp.concatenate(
        [jnp.concatenate([head(r, 4 * k + j) for r in (q_ref, c_ref) for k in range(4)], axis=1) for j in range(4)],
        axis=0,
    )
    for g in range(2):
        slab = dot(place(base[g], 4), full).astype(bf16)
        out_ref[:, g * 512:(g + 1) * 512] = slab[:, :512]
        out_ref[:, 1280 + g * 512:1280 + (g + 1) * 512] = slab[:, 512:]
    last = jnp.concatenate(
        [
            jnp.concatenate([head(r, 4 * (2 * kp + kk) + j) for r in (q_ref, c_ref) for kp in range(2)], axis=1)
            for kk in range(2)
            for j in range(4)
        ],
        axis=0,
    )
    slab = dot(place(base[2], 8), last).astype(bf16)
    out_ref[:, 1024:1280] = slab[:, :256]
    out_ref[:, 2304:2560] = slab[:, 256:]


def unpack_kernel(row_ref, col_ref, in_ref, out_ref):
    col = col_ref[...]
    same = jnp.broadcast_to(col, (TOK, TOK)) == jnp.broadcast_to(row_ref[...], (TOK, TOK))
    before = iota((TOK, TOK), 1) < iota((TOK, TOK), 0)
    rank = jnp.sum(jnp.where(same & before, 1, 0), axis=1, keepdims=True)
    base = bases(col, rank)
    slab_col = iota((TOK, SLAB), 1)

    def pick(first, count):
        wide = jnp.broadcast_to(first, (TOK, SLAB))
        return jnp.concatenate([one_hot(slab_col == wide + j) for j in range(count)], axis=0)

    total = None
    for g in range(2):
        slab = jnp.concatenate([in_ref[:, g * 256:(g + 1) * 256], in_ref[:, 640 + g * 256:640 + (g + 1) * 256]], axis=1)
        part = dot(pick(base[g], 4), slab)
        total = part if total is None else total + part
    last = dot(pick(base[2], 8), jnp.concatenate([in_ref[:, 512:640], in_ref[:, 1152:1280]], axis=1))
    for k in range(4):
        for j in range(4):
            h = 4 * k + j
            first = ((k % 2) * 4 + j) * TOK
            value = total[j * TOK:(j + 1) * TOK, k * 128:(k + 1) * 128]
            value = value + last[first:first + TOK, (k // 2) * 128:(k // 2 + 1) * 128]
            out_ref[:, h * HEAD_DIM:(h + 1) * HEAD_DIM] = value.astype(bf16)


def attend(group, rolled, z, recv_ref, kv_ref, out_ref, out_lane, grad_ref, q_s, c_s, qt_s, ct_s, s_s, w_s, acc_s):
    half_row = iota((SLAB // 2, SLAB), 0)
    half_col = iota((SLAB // 2, SLAB), 1)
    back_row = iota((SLAB, SLAB // 2), 0)
    back_col = iota((SLAB, SLAB // 2), 1)
    tail = None
    for kk in range(2):
        k = 2 * group + kk
        take = one_hot(half_col == (half_row // 4) * 8 + kk * 4 + half_row % 4)
        give = one_hot(back_row == (back_col // 4) * 8 + kk * 4 + back_col % 4)
        for ref, first in ((q_s, 0), (c_s, 1280)):
            ref[0:256, :] = recv_ref[:, first + k * 128:first + (k + 1) * 128]
            ref[256:512, :] = recv_ref[:, first + 512 + k * 128:first + 512 + (k + 1) * 128]
            ref[512:640, :] = dot(take, recv_ref[:, first + 1024 + group * 128:first + 1024 + (group + 1) * 128]).astype(bf16)
        qt_s[...] = q_s[...].astype(f32).T.astype(bf16)
        key = slice(kk * 128, (kk + 1) * 128)
        val = slice(256 + kk * 128, 256 + (kk + 1) * 128)

        def score_step(i, top):
            rows = pl.ds(pl.multiple_of(i * BLOCK, BLOCK), BLOCK)
            s = dot(kv_ref[rows, key], qt_s[...])
            s_s[rows, :] = s
            return jnp.maximum(top, jnp.max(s, axis=0, keepdims=True))

        top = lax.fori_loop(0, ROWS // BLOCK, score_step, jnp.full((1, QUERIES), -jnp.inf, f32))
        top = top * EXP2_SCALE
        acc_s[...] = jnp.zeros_like(acc_s)

        def weight_step(i, total):
            rows = pl.ds(pl.multiple_of(i * BLOCK, BLOCK), BLOCK)
            w = jnp.exp2(s_s[rows, :] * EXP2_SCALE - top)
            wb = w.astype(bf16)
            w_s[rows, :] = wb
            vt = kv_ref[rows, val].astype(f32).T.astype(bf16)
            acc_s[...] += dot(vt, wb)
            return total + jnp.sum(w, axis=0, keepdims=True)

        total = lax.fori_loop(0, ROWS // BLOCK, weight_step, jnp.zeros((1, QUERIES), f32))
        inverse = 1.0 / total
        out_t = acc_s[...] * inverse
        ct = (c_s[...].astype(f32).T * inverse).astype(bf16)
        ct_s[...] = ct
        delta = jnp.sum(ct.astype(f32) * out_t, axis=0, keepdims=True)
        c_s[...] = ct.astype(f32).T.astype(bf16)
        out = out_t.T.astype(bf16)
        out_ref[:, out_lane + kk * 128:out_lane + (kk + 1) * 128] = out[0:256, :]
        out_ref[:, out_lane + 256 + kk * 128:out_lane + 256 + (kk + 1) * 128] = out[256:512, :]
        part = dot(give, out[512:640, :])
        tail = part if tail is None else tail + part

        def grad_step(i, carry):
            rows = pl.ds(pl.multiple_of(i * BLOCK, BLOCK), BLOCK)
            wb = w_s[rows, :]
            prob_grad = dot(kv_ref[rows, val], ct_s[...])
            ds = (wb.astype(f32) * (prob_grad - delta)).astype(bf16)
            value_grad = dot(wb, c_s[...]).astype(bf16)
            key_grad = (dot(ds, q_s[...]) * SCALE).astype(bf16)
            for sub in range(BLOCK // SHARD):
                at = i * (BLOCK // SHARD) + sub
                if rolled:
                    at = lax.rem(at - z + RING, RING)
                to = pl.ds(pl.multiple_of(at * SHARD, SHARD), SHARD)
                grad_ref[to, key] = key_grad[sub * SHARD:(sub + 1) * SHARD, :]
                grad_ref[to, val] = value_grad[sub * SHARD:(sub + 1) * SHARD, :]
            return carry

        lax.fori_loop(0, ROWS // BLOCK, grad_step, 0)
    out_ref[:, out_lane + 512:out_lane + 640] = tail.astype(bf16)


def first_kernel(offsets, z_ref, recv_ref, *refs):
    blocks = refs[:RING]
    out_ref, grad_ref, kv_s = refs[RING:RING + 3]
    z = z_ref[0]
    for offset, block in zip(offsets, blocks):
        at = lax.rem(z + (offset + RING), RING)
        kv_s[pl.ds(pl.multiple_of(at * SHARD, SHARD), SHARD), :] = block[...]
    attend(0, False, z, recv_ref, kv_s, out_ref, 0, grad_ref, *refs[RING + 3:])


def second_kernel(z_ref, recv_ref, kv_ref, early_ref, out_ref, grad_ref, *scratch):
    out_ref[:, 0:640] = early_ref[...]
    attend(1, True, z_ref[0], recv_ref, kv_ref, out_ref, 640, grad_ref, *scratch)


def vmem(count):
    return [pl.BlockSpec(memory_space=pltpu.VMEM)] * count


SMEM = pl.BlockSpec(memory_space=pltpu.SMEM)
WORK = [
    pltpu.VMEM((QUERIES, HEAD_DIM), bf16),
    pltpu.VMEM((QUERIES, HEAD_DIM), bf16),
    pltpu.VMEM((HEAD_DIM, QUERIES), bf16),
    pltpu.VMEM((HEAD_DIM, QUERIES), bf16),
    pltpu.VMEM((ROWS, QUERIES), f32),
    pltpu.VMEM((ROWS, QUERIES), bf16),
    pltpu.VMEM((HEAD_DIM, QUERIES), f32),
]
PARAMS = pltpu.CompilerParams(vmem_limit_bytes=VMEM_LIMIT)
ATTEND_COST = pl.CostEstimate(
    flops=2 * 5 * 2 * QUERIES * ROWS * HEAD_DIM * 2, bytes_accessed=6 * 1024 * 1024, transcendentals=2 * QUERIES * ROWS
)
SMALL_COST = pl.CostEstimate(flops=2 * 1024 * 1024 * 1024, bytes_accessed=3 * 1024 * 1024, transcendentals=0)


def local(queries, cotangent, corpus_of, cartridge):
    forward = [(i, (i + 1) % RING) for i in range(RING)]
    backward = [(i, (i - 1) % RING) for i in range(RING)]
    z = lax.axis_index("conv").astype(jnp.int32).reshape(1)
    shard = cartridge[0]
    shard_a = jnp.concatenate([shard[:, 0:256], shard[:, 512:768]], axis=1)
    shard_b = jnp.concatenate([shard[:, 256:512], shard[:, 768:1024]], axis=1)
    gathered_b = lax.all_gather(shard_b, "conv", axis=0, tiled=True)

    col = corpus_of.astype(jnp.int32)
    row = col.reshape(1, TOK)
    packed = pl.pallas_call(
        pack_kernel,
        out_shape=jax.ShapeDtypeStruct((SLAB, 2560), bf16),
        in_specs=vmem(4),
        out_specs=vmem(1)[0],
        compiler_params=PARAMS,
        cost_estimate=SMALL_COST,
        name="pack",
    )(row, col, queries, cotangent)
    recv = lax.all_to_all(packed, "corpus", split_axis=0, concat_axis=0, tiled=True)

    blocks = [shard_a]
    offsets = [0]
    ahead = behind = shard_a
    for step in range(1, RING // 2 + 1):
        if step == RECV_STEP:
            ahead, behind, recv = lax.optimization_barrier((ahead, behind, recv))
        ahead = lax.ppermute(ahead, "conv", forward)
        blocks.append(ahead)
        offsets.append(-step)
        if step < RING // 2:
            behind = lax.ppermute(behind, "conv", backward)
            blocks.append(behind)
            offsets.append(step)

    out_a, grad_a = pl.pallas_call(
        functools.partial(first_kernel, tuple(offsets)),
        out_shape=(jax.ShapeDtypeStruct((SLAB, 640), bf16), jax.ShapeDtypeStruct((ROWS, 512), bf16)),
        in_specs=[SMEM] + vmem(1 + RING),
        out_specs=tuple(vmem(2)),
        scratch_shapes=[pltpu.VMEM((ROWS, 512), bf16)] + WORK,
        compiler_params=PARAMS,
        cost_estimate=ATTEND_COST,
        name="attend_a",
    )(z, recv, *blocks)
    done_a = lax.psum_scatter(grad_a, "conv", scatter_dimension=0, tiled=True)

    out, grad_b = pl.pallas_call(
        second_kernel,
        out_shape=(jax.ShapeDtypeStruct((SLAB, 1280), bf16), jax.ShapeDtypeStruct((ROWS, 512), bf16)),
        in_specs=[SMEM] + vmem(3),
        out_specs=tuple(vmem(2)),
        scratch_shapes=WORK,
        compiler_params=PARAMS,
        cost_estimate=ATTEND_COST,
        name="attend_b",
    )(z, recv, gathered_b, out_a)

    def piece(index):
        return grad_b[index * SHARD:(index + 1) * SHARD, :].astype(f32)

    up = piece(8).astype(bf16)
    down = piece(9).astype(bf16)
    for step in range(1, RING // 2 + 1):
        if step == DONE_STEP:
            up, down, done_a = lax.optimization_barrier((up, down, done_a))
        up = lax.ppermute(up, "conv", forward)
        if step < RING // 2:
            up = (up.astype(f32) + piece(8 - step)).astype(bf16)
            down = lax.ppermute(down, "conv", backward)
            if step < RING // 2 - 1:
                down = (down.astype(f32) + piece(9 + step)).astype(bf16)
    done_b = piece(0) + up.astype(f32) + down.astype(f32)

    replies = lax.all_to_all(out, "corpus", split_axis=0, concat_axis=0, tiled=True)
    attended = pl.pallas_call(
        unpack_kernel,
        out_shape=jax.ShapeDtypeStruct((TOK, 2048), bf16),
        in_specs=vmem(3),
        out_specs=vmem(1)[0],
        compiler_params=PARAMS,
        cost_estimate=SMALL_COST,
        name="unpack",
    )(row, col, replies)
    done_a = done_a.astype(f32)
    grad = jnp.concatenate([done_a[:, 0:256], done_b[:, 0:256], done_a[:, 256:512], done_b[:, 256:512]], axis=1)
    return attended, grad[None]


def solution(mesh):
    return jax.shard_map(
        local,
        mesh=mesh,
        in_specs=(
            P(("corpus", "conv"), None),
            P(("corpus", "conv"), None),
            P(("corpus", "conv"), None),
            P("corpus", "conv", None),
        ),
        out_specs=(P(("corpus", "conv"), None), P("corpus", "conv", None)),
        check_vma=False,
    )
```

time: 256 us -> 244 us (0.953)
  starting transfers between devices: 23.7 us -> 121 us
  waiting for transfers between devices: 121 us -> 59.1 us
  matrix products: 52.4 us -> 0 us
  Pallas kernels: 0 us -> 39.2 us
  local copies, waits for them, and re-layouts: 26.9 us -> 4.96 us
  other arithmetic: 16.3 us -> 3.94 us
    ppermute x0 -> x30, starting transfers between devices: none -> 101 us  [the longest x7 41.8 us: local(): behind = lax.ppermute(behind, 'conv', backward)]
    ppermute x0 -> x30, waiting for transfers between devices: none -> 59 us  [the longest x8 22.4 us: local(): up = lax.ppermute(up, 'conv', forward)]
    unnamed x3 -> x2, waiting for transfers between devices: 50.2 us -> 0.03 us
    pallas_call x0 -> x4, Pallas kernels: none -> 39.2 us  [the longest x1 16.5 us: local(): pl.pallas_call(second_kernel, out_shape=(jax.ShapeDtypeStruct((SLAB, 1280...]
    all_to_all x3 -> x2, waiting for transfers between devices: 38.8 us -> 0.01 us  [the longest x1 0.01 us: local(): lax.all_to_all(out, 'corpus', split_axis=0, concat_axis=0, tiled=True)]
    all_gather x1, waiting for transfers between devices: 32.4 us -> 0.02 us  [local(): gathered_b = lax.all_gather(shard_b, 'conv', axis=0, tiled=True)]
    dot_general x12 -> x0, matrix products: 31.3 us -> none  [the longest x4 15.3 us: local(): jnp.einsum('sgr,sgd->rd', score_grad, query_heads[:, head], preferred_ele...]
    sub x4 -> x0, matrix products: 21.1 us -> none  [local(): weights = jnp.exp(scores - row_max)]
  transfers between devices with their start and end apart: 5 -> 34, of which waited for: 5 -> 24; matrix products, arithmetic and copies ran while one was open for 5% -> 2% of each run, Pallas kernels for 0% -> 16%
where the time goes in v1:
time: 244 us; the launch traced here: 243 us
  starting transfers between devices  121 us (50%)
  waiting for transfers between devices  59.1 us (24%)
  Pallas kernels  39.2 us (16%)
  between operations  14.6 us (6%)
  local copies, waits for them, and re-layouts  4.96 us (2%)
  other arithmetic  3.94 us (2%)
    ppermute x7, starting transfers between devices, local(): behind = lax.ppermute(behind, 'conv', backward)  41.8 us
    ppermute x8, starting transfers between devices, local(): up = lax.ppermute(up, 'conv', forward)  24.3 us
    ppermute x8, waiting for transfers between devices, local(): up = lax.ppermute(up, 'conv', forward)  22.4 us
    ppermute x8, waiting for transfers between devices, local(): ahead = lax.ppermute(ahead, 'conv', forward)  20.3 us
    ppermute x7, starting transfers between devices, local(): down = lax.ppermute(down, 'conv', backward)  19.7 us
    pallas_call x1, Pallas kernels, local(): pl.pallas_call(second_kernel, out_shape=(jax.ShapeDtypeStruct((SLAB, 1280...  16.5 us
    pallas_call x1, Pallas kernels, local(): pl.pallas_call(functools.partial(first_kernel, tuple(offsets)), out_shape...  16.4 us
    ppermute x8, starting transfers between devices, local(): ahead = lax.ppermute(ahead, 'conv', forward)  15.3 us
  transfers between devices with their start and end apart: 34, of which 24 were waited for; matrix products, arithmetic and copies ran while one was open for 2% of the time, Pallas kernels for 16%

profile of v1, /device:TPU:6, one launch (start us, length us, event | category | flops | bytes accessed | tf_op | source)
XLA Modules:
  0.0 243.1 jit_solution(4992881464495800525)
XLA Ops:
  10.2 3.4 %pack.1 = bf16[256,2560]{1,0:T(8,128)(2,1)} custom-call(s32[1,128]{1,0:T(1,128)} %bitcast.14, s32[128,1]{1,0:T(8,128)} %copy.7.col_ref, bf16[128,2048]{1,0:T(8,128)(2,1)} %q_ref.1, bf16[128,2048]{1,0:T(8,128)(2,1)} %c_ref.1), custom_call_target="tpu_custom_call" | custom-call | flops 2147483648 | bytes 3145728 | tf_op jit(solution)/shard_map/pack/pallas_call | solution.py:233
  13.6 9.5 %all-to-all-start = ((bf16[32,8,2560]{2,1,0:T(8,128)(2,1)}), bf16[32,8,2560]{2,1,0:T(8,128)(2,1)S(1)}, u32[]{:S(2)}, u32[]{:S(2)}) async-start(bf16[32,8,2560]{2,1,0:T(8,128)(2,1)} %bitcast.11), calls=%async_computation | async-start | bytes 2621440 | tf_op jit(solution)/shard_map/all_to_all | solution.py:242
  23.2 9.5 %collective-permute-start.4 = (bf16[128,512]{1,0:T(8,128)(2,1)S(1)}, bf16[128,512]{1,0:T(8,128)(2,1)S(1)}, u32[]{:S(2)}, u32[]{:S(2)}) collective-permute-start(bf16[128,512]{1,0:T(8,128)(2,1)S(1)} %pad_maximum_fusion.refs_0_), channel_id=1, source_target_pairs={{0,15},{1,0},{2,1},{3,2},{4,3},{5,4},{6,5},{7,6},{8,7},{9,8},{10,9... | collective-permute-start | bytes 393224 | tf_op jit(solution)/shard_map/ppermute | solution.py:254
  35.7 5.6 %collective-permute-start.5 = (bf16[128,512]{1,0:T(8,128)(2,1)S(1)}, bf16[128,512]{1,0:T(8,128)(2,1)S(1)}, u32[]{:S(2)}, u32[]{:S(2)}) collective-permute-start(bf16[128,512]{1,0:T(8,128)(2,1)S(1)} %collective-permute-done.4.refs_2_), channel_id=1, source_target_pairs={{0,15},{1,0},{2,1},{3,2},{4,3},{5,4},{6,5},{7,6},{8,7},{9,8},{10,9... | collective-permute-start | bytes 393224 | tf_op jit(solution)/shard_map/ppermute | solution.py:254
  45.5 5.6 %collective-permute-start.6 = (bf16[128,512]{1,0:T(8,128)(2,1)S(1)}, bf16[128,512]{1,0:T(8,128)(2,1)S(1)}, u32[]{:S(2)}, u32[]{:S(2)}) collective-permute-start(bf16[128,512]{1,0:T(8,128)(2,1)S(1)} %collective-permute-done.5.refs_4_), channel_id=1, source_target_pairs={{0,15},{1,0},{2,1},{3,2},{4,3},{5,4},{6,5},{7,6},{8,7},{9,8},{10,9... | collective-permute-start | bytes 393224 | tf_op jit(solution)/shard_map/ppermute | solution.py:254
  54.4 5.7 %collective-permute-start.7 = (bf16[128,512]{1,0:T(8,128)(2,1)S(1)}, bf16[128,512]{1,0:T(8,128)(2,1)S(1)}, u32[]{:S(2)}, u32[]{:S(2)}) collective-permute-start(bf16[128,512]{1,0:T(8,128)(2,1)S(1)} %collective-permute-done.6.refs_6_), channel_id=1, source_target_pairs={{0,15},{1,0},{2,1},{3,2},{4,3},{5,4},{6,5},{7,6},{8,7},{9,8},{10,9... | collective-permute-start | bytes 393224 | tf_op jit(solution)/shard_map/ppermute | solution.py:254
  63.6 6.8 %collective-permute-done.3.refs_7_ = bf16[128,512]{1,0:T(8,128)(2,1)S(1)} collective-permute-done((bf16[128,512]{1,0:T(8,128)(2,1)S(1)}, bf16[128,512]{1,0:T(8,128)(2,1)S(1)}, u32[]{:S(2)}, u32[]{:S(2)}) %collective-permute-start.3) | collective-permute-done | bytes 131104 | tf_op jit(solution)/shard_map/ppermute | solution.py:250
  72.4 5.1 %collective-permute-start.9 = (bf16[128,512]{1,0:T(8,128)(2,1)S(1)}, bf16[128,512]{1,0:T(8,128)(2,1)S(1)}, u32[]{:S(2)}, u32[]{:S(2)}) collective-permute-start(bf16[128,512]{1,0:T(8,128)(2,1)S(1)} %collective-permute-done.7.refs_8_), channel_id=1, source_target_pairs={{0,15},{1,0},{2,1},{3,2},{4,3},{5,4},{6,5},{7,6},{8,7},{9,8},{10,9... | collective-permute-start | bytes 393224 | tf_op jit(solution)/shard_map/ppermute | solution.py:254
  81.2 5.1 %collective-permute-start.11 = (bf16[128,512]{1,0:T(8,128)(2,1)S(1)}, bf16[128,512]{1,0:T(8,128)(2,1)S(1)}, u32[]{:S(2)}, u32[]{:S(2)}) collective-permute-start(bf16[128,512]{1,0:T(8,128)(2,1)S(1)} %collective-permute-done.9.refs_10_), channel_id=1, source_target_pairs={{0,15},{1,0},{2,1},{3,2},{4,3},{5,4},{6,5},{7,6},{8,7},{9,8},{10,9... | collective-permute-start | bytes 393224 | tf_op jit(solution)/shard_map/ppermute | solution.py:254
  89.7 5.1 %collective-permute-start.13 = (bf16[128,512]{1,0:T(8,128)(2,1)S(1)}, bf16[128,512]{1,0:T(8,128)(2,1)S(1)}, u32[]{:S(2)}, u32[]{:S(2)}) collective-permute-start(bf16[128,512]{1,0:T(8,128)(2,1)S(1)} %collective-permute-done.11.refs_12_), channel_id=1, source_target_pairs={{0,15},{1,0},{2,1},{3,2},{4,3},{5,4},{6,5},{7,6},{8,7},{9,8},{10,9... | collective-permute-start | bytes 393224 | tf_op jit(solution)/shard_map/ppermute | solution.py:254
  97.9 6.1 %collective-permute-done.14.refs_15_ = bf16[128,512]{1,0:T(8,128)(2,1)S(1)} collective-permute-done((bf16[128,512]{1,0:T(8,128)(2,1)S(1)}, bf16[128,512]{1,0:T(8,128)(2,1)S(1)}, u32[]{:S(2)}, u32[]{:S(2)}) %collective-permute-start.14) | collective-permute-done | bytes 131104 | tf_op jit(solution)/shard_map/ppermute | solution.py:250
  104.6 16.4 %attend_a.1 = (bf16[256,640]{1,0:T(8,128)(2,1)}, bf16[2048,512]{1,0:T(8,128)(2,1)}) custom-call(s32[1]{0:T(128)} %bitcast.1.z_ref, bf16[256,2560]{1,0:T(8,128)(2,1)} %bitcast.9, bf16[128,512]{1,0:T(8,128)(2,1)} %copy-done.4, bf16[128,512]{1,0:T(8,128)(2,1)} %copy-done.6, bf16[128,512]{1,0:T(8,128)(2,1)} %copy-done.5, bf16[128,512]{1,0:T(8,128)(2,1)} %copy-done.8, ...), custom_call_target="tpu_custom_call" | custom-call | flops 6710886400 | bytes 6291456 | tf_op jit(solution)/shard_map/attend_a/pallas_call | solution.py:258
  121.1 16.5 %attend_b.1 = (bf16[256,1280]{1,0:T(8,128)(2,1)}, bf16[2048,512]{1,0:T(8,128)(2,1)}) custom-call(s32[1]{0:T(128)} %bitcast.1.z_ref, bf16[256,2560]{1,0:T(8,128)(2,1)} %bitcast.10, bf16[2048,512]{1,0:T(8,128)(2,1)} %all-gather.2.cloned.1.call-done.kv_ref, bf16[256,640]{1,0:T(8,128)(2,1)} %get-tuple-element.15.early_ref), custom_call_target="tpu_custom_call" | custom-call | flops 6710886400 | bytes 6291456 | tf_op jit(solution)/shard_map/attend_b/pallas_call | solution.py:270
  140.7 3.9 %collective-permute-start.15 = (bf16[128,512]{1,0:T(8,128)(2,1)S(1)}, bf16[128,512]{1,0:T(8,128)(2,1)S(1)}, u32[]{:S(2)}, u32[]{:S(2)}) collective-permute-start(bf16[128,512]{1,0:T(8,128)(2,1)S(1)} %get-tuple-element.35), channel_id=1, source_target_pairs={{0,1},{1,2},{2,3},{3,4},{4,5},{5,6},{6,7},{7,8},{8,9},{9,10},{10,1... | collective-permute-start | bytes 393224 | tf_op jit(solution)/shard_map/ppermute | solution.py:289
  152.6 3.9 %collective-permute-start.16 = (bf16[128,512]{1,0:T(8,128)(2,1)S(1)}, bf16[128,512]{1,0:T(8,128)(2,1)S(1)}, u32[]{:S(2)}, u32[]{:S(2)}) collective-permute-start(bf16[128,512]{1,0:T(8,128)(2,1)S(1)} %get-tuple-element.33), channel_id=1, source_target_pairs={{0,1},{1,2},{2,3},{3,4},{4,5},{5,6},{6,7},{7,8},{8,9},{9,10},{10,1... | collective-permute-start | bytes 393224 | tf_op jit(solution)/shard_map/ppermute | solution.py:289
  168.3 3.2 %collective-permute-done.23 = bf16[128,512]{1,0:T(8,128)(2,1)S(1)} collective-permute-done((bf16[128,512]{1,0:T(8,128)(2,1)S(1)}, bf16[128,512]{1,0:T(8,128)(2,1)S(1)}, u32[]{:S(2)}, u32[]{:S(2)}) %collective-permute-start.23) | collective-permute-done | bytes 131104 | tf_op jit(solution)/shard_map/ppermute | solution.py:292
  171.5 5.5 %collective-permute-done.17 = bf16[128,512]{1,0:T(8,128)(2,1)S(1)} collective-permute-done((bf16[128,512]{1,0:T(8,128)(2,1)S(1)}, bf16[128,512]{1,0:T(8,128)(2,1)S(1)}, u32[]{:S(2)}, u32[]{:S(2)}) %collective-permute-start.17) | collective-permute-done | bytes 131104 | tf_op jit(solution)/shard_map/ppermute | solution.py:289
  179.0 3.9 %collective-permute-start.18 = (bf16[128,512]{1,0:T(8,128)(2,1)S(1)}, bf16[128,512]{1,0:T(8,128)(2,1)S(1)}, u32[]{:S(2)}, u32[]{:S(2)}) collective-permute-start(bf16[128,512]{1,0:T(8,128)(2,1)S(1)} %get-tuple-element.29), channel_id=1, source_target_pairs={{0,1},{1,2},{2,3},{3,4},{4,5},{5,6},{6,7},{7,8},{8,9},{9,10},{10,1... | collective-permute-start | bytes 393224 | tf_op jit(solution)/shard_map/ppermute | solution.py:289
  190.8 3.2 %collective-permute-start.19 = (bf16[128,512]{1,0:T(8,128)(2,1)S(1)}, bf16[128,512]{1,0:T(8,128)(2,1)S(1)}, u32[]{:S(2)}, u32[]{:S(2)}) collective-permute-start(bf16[128,512]{1,0:T(8,128)(2,1)S(1)} %get-tuple-element.27), channel_id=1, source_target_pairs={{0,1},{1,2},{2,3},{3,4},{4,5},{5,6},{6,7},{7,8},{8,9},{9,10},{10,1... | collective-permute-start | bytes 393224 | tf_op jit(solution)/shard_map/ppermute | solution.py:289
  194.0 10.7 %all-to-all-start.1 = ((bf16[32,8,1280]{2,1,0:T(8,128)(2,1)}), bf16[32,8,1280]{2,1,0:T(8,128)(2,1)S(1)}, u32[]{:S(2)}, u32[]{:S(2)}) async-start(bf16[32,8,1280]{2,1,0:T(8,128)(2,1)} %bitcast.5), calls=%async_computation.1 | async-start | bytes 1310720 | tf_op jit(solution)/shard_map/all_to_all | solution.py:297
  204.8 3.1 %collective-permute-start.26 = (bf16[128,512]{1,0:T(8,128)(2,1)S(1)}, bf16[128,512]{1,0:T(8,128)(2,1)S(1)}, u32[]{:S(2)}, u32[]{:S(2)}) collective-permute-start(bf16[128,512]{1,0:T(8,128)(2,1)S(1)} %get-tuple-element.24), channel_id=1, source_target_pairs={{0,15},{1,0},{2,1},{3,2},{4,3},{5,4},{6,5},{7,6},{8,7},{9,8},{10,9... | collective-permute-start | bytes 393224 | tf_op jit(solution)/shard_map/ppermute | solution.py:292
  212.3 4.1 %collective-permute-done.20 = bf16[128,512]{1,0:T(8,128)(2,1)S(1)} collective-permute-done((bf16[128,512]{1,0:T(8,128)(2,1)S(1)}, bf16[128,512]{1,0:T(8,128)(2,1)S(1)}, u32[]{:S(2)}, u32[]{:S(2)}) %collective-permute-start.20) | collective-permute-done | bytes 131104 | tf_op jit(solution)/shard_map/ppermute | solution.py:289
  222.1 5.1 %collective-permute-start.29 = (bf16[128,512]{1,0:T(8,128)(2,1)S(1)}, bf16[128,512]{1,0:T(8,128)(2,1)S(1)}, u32[]{:S(2)}, u32[]{:S(2)}) collective-permute-start(bf16[128,512]{1,0:T(8,128)(2,1)S(1)} %get-tuple-element.21), channel_id=1, source_target_pairs={{0,15},{1,0},{2,1},{3,2},{4,3},{5,4},{6,5},{7,6},{8,7},{9,8},{10,9... | collective-permute-start | bytes 393224 | tf_op jit(solution)/shard_map/ppermute | solution.py:292
  229.7 5.6 %collective-permute-done.28 = bf16[128,512]{1,0:T(8,128)(2,1)S(1)} collective-permute-done((bf16[128,512]{1,0:T(8,128)(2,1)S(1)}, bf16[128,512]{1,0:T(8,128)(2,1)S(1)}, u32[]{:S(2)}, u32[]{:S(2)}) %collective-permute-start.28) | collective-permute-done | bytes 131104 | tf_op jit(solution)/shard_map/ppermute | solution.py:289
  (106 shorter events, 75.6 us)
Async XLA Ops:
  7.2 114.0 %all-gather.2.cloned.1.call-start = ((), (), s32[]{:S(2)}) async-start(), calls=%async_computation.3 | async-start | bytes 2228224 | tf_op jit(solution)/shard_map/all_gather | solution.py:229
  13.6 56.8 %all-to-all-start = ((bf16[32,8,2560]{2,1,0:T(8,128)(2,1)}), bf16[32,8,2560]{2,1,0:T(8,128)(2,1)S(1)}, u32[]{:S(2)}, u32[]{:S(2)}) async-start(bf16[32,8,2560]{2,1,0:T(8,128)(2,1)} %bitcast.11), calls=%async_computation | async-start | bytes 2621440 | tf_op jit(solution)/shard_map/all_to_all | solution.py:242
  23.1 193.3 %reduce-scatter.2.cloned.1.call-start = ((), (), s32[]{:S(2)}) async-start(), calls=%async_computation.4 | async-start | bytes 2228224 | tf_op jit(solution)/shard_map/reduce_scatter | solution.py:268
  23.2 12.5 %collective-permute-start.4 = (bf16[128,512]{1,0:T(8,128)(2,1)S(1)}, bf16[128,512]{1,0:T(8,128)(2,1)S(1)}, u32[]{:S(2)}, u32[]{:S(2)}) collective-permute-start(bf16[128,512]{1,0:T(8,128)(2,1)S(1)} %pad_maximum_fusion.refs_0_), channel_id=1, source_target_pairs={{0,15},{1,0},{2,1},{3,2},{4,3},{5,4},{6,5},{7,6},{8,7},{9,8},{10,9... | collective-permute-start | bytes 393224 | tf_op jit(solution)/shard_map/ppermute | solution.py:254
  32.7 10.1 %collective-permute-start = (bf16[128,512]{1,0:T(8,128)(2,1)S(1)}, bf16[128,512]{1,0:T(8,128)(2,1)S(1)}, u32[]{:S(2)}, u32[]{:S(2)}) collective-permute-start(bf16[128,512]{1,0:T(8,128)(2,1)S(1)} %pad_maximum_fusion.refs_0_), channel_id=1, source_target_pairs={{0,1},{1,2},{2,3},{3,4},{4,5},{5,6},{6,7},{7,8},{8,9},{9,10},{10,1... | collective-permute-start | bytes 393224 | tf_op jit(solution)/shard_map/ppermute | solution.py:250
  35.7 9.7 %collective-permute-start.5 = (bf16[128,512]{1,0:T(8,128)(2,1)S(1)}, bf16[128,512]{1,0:T(8,128)(2,1)S(1)}, u32[]{:S(2)}, u32[]{:S(2)}) collective-permute-start(bf16[128,512]{1,0:T(8,128)(2,1)S(1)} %collective-permute-done.4.refs_2_), channel_id=1, source_target_pairs={{0,15},{1,0},{2,1},{3,2},{4,3},{5,4},{6,5},{7,6},{8,7},{9,8},{10,9... | collective-permute-start | bytes 393224 | tf_op jit(solution)/shard_map/ppermute | solution.py:254
  42.8 8.9 %collective-permute-start.1 = (bf16[128,512]{1,0:T(8,128)(2,1)S(1)}, bf16[128,512]{1,0:T(8,128)(2,1)S(1)}, u32[]{:S(2)}, u32[]{:S(2)}) collective-permute-start(bf16[128,512]{1,0:T(8,128)(2,1)S(1)} %collective-permute-done.refs_1_), channel_id=1, source_target_pairs={{0,1},{1,2},{2,3},{3,4},{4,5},{5,6},{6,7},{7,8},{8,9},{9,10},{10,1... | collective-permute-start | bytes 393224 | tf_op jit(solution)/shard_map/ppermute | solution.py:250
  45.5 8.9 %collective-permute-start.6 = (bf16[128,512]{1,0:T(8,128)(2,1)S(1)}, bf16[128,512]{1,0:T(8,128)(2,1)S(1)}, u32[]{:S(2)}, u32[]{:S(2)}) collective-permute-start(bf16[128,512]{1,0:T(8,128)(2,1)S(1)} %collective-permute-done.5.refs_4_), channel_id=1, source_target_pairs={{0,15},{1,0},{2,1},{3,2},{4,3},{5,4},{6,5},{7,6},{8,7},{9,8},{10,9... | collective-permute-start | bytes 393224 | tf_op jit(solution)/shard_map/ppermute | solution.py:254
  51.7 9.4 %collective-permute-start.2 = (bf16[128,512]{1,0:T(8,128)(2,1)S(1)}, bf16[128,512]{1,0:T(8,128)(2,1)S(1)}, u32[]{:S(2)}, u32[]{:S(2)}) collective-permute-start(bf16[128,512]{1,0:T(8,128)(2,1)S(1)} %collective-permute-done.1.refs_3_), channel_id=1, source_target_pairs={{0,1},{1,2},{2,3},{3,4},{4,5},{5,6},{6,7},{7,8},{8,9},{9,10},{10,1... | collective-permute-start | bytes 393224 | tf_op jit(solution)/shard_map/ppermute | solution.py:250
  54.4 9.2 %collective-permute-start.7 = (bf16[128,512]{1,0:T(8,128)(2,1)S(1)}, bf16[128,512]{1,0:T(8,128)(2,1)S(1)}, u32[]{:S(2)}, u32[]{:S(2)}) collective-permute-start(bf16[128,512]{1,0:T(8,128)(2,1)S(1)} %collective-permute-done.6.refs_6_), channel_id=1, source_target_pairs={{0,15},{1,0},{2,1},{3,2},{4,3},{5,4},{6,5},{7,6},{8,7},{9,8},{10,9... | collective-permute-start | bytes 393224 | tf_op jit(solution)/shard_map/ppermute | solution.py:254
  61.1 9.3 %collective-permute-start.3 = (bf16[128,512]{1,0:T(8,128)(2,1)S(1)}, bf16[128,512]{1,0:T(8,128)(2,1)S(1)}, u32[]{:S(2)}, u32[]{:S(2)}) collective-permute-start(bf16[128,512]{1,0:T(8,128)(2,1)S(1)} %collective-permute-done.2.refs_5_), channel_id=1, source_target_pairs={{0,1},{1,2},{2,3},{3,4},{4,5},{5,6},{6,7},{7,8},{8,9},{9,10},{10,1... | collective-permute-start | bytes 393224 | tf_op jit(solution)/shard_map/ppermute | solution.py:250
  70.4 8.9 %collective-permute-start.8 = (bf16[128,512]{1,0:T(8,128)(2,1)S(1)}, bf16[128,512]{1,0:T(8,128)(2,1)S(1)}, u32[]{:S(2)}, u32[]{:S(2)}) collective-permute-start(bf16[128,512]{1,0:T(8,128)(2,1)S(1)} %collective-permute-done.3.refs_7_), channel_id=1, source_target_pairs={{0,1},{1,2},{2,3},{3,4},{4,5},{5,6},{6,7},{7,8},{8,9},{9,10},{10,1... | collective-permute-start | bytes 393224 | tf_op jit(solution)/shard_map/ppermute | solution.py:250
  72.4 8.9 %collective-permute-start.9 = (bf16[128,512]{1,0:T(8,128)(2,1)S(1)}, bf16[128,512]{1,0:T(8,128)(2,1)S(1)}, u32[]{:S(2)}, u32[]{:S(2)}) collective-permute-start(bf16[128,512]{1,0:T(8,128)(2,1)S(1)} %collective-permute-done.7.refs_8_), channel_id=1, source_target_pairs={{0,15},{1,0},{2,1},{3,2},{4,3},{5,4},{6,5},{7,6},{8,7},{9,8},{10,9... | collective-permute-start | bytes 393224 | tf_op jit(solution)/shard_map/ppermute | solution.py:254
  138.8 8.5 %collective-permute-start.21 = (bf16[128,512]{1,0:T(8,128)(2,1)S(1)}, bf16[128,512]{1,0:T(8,128)(2,1)S(1)}, u32[]{:S(2)}, u32[]{:S(2)}) collective-permute-start(bf16[128,512]{1,0:T(8,128)(2,1)S(1)} %get-tuple-element.34), channel_id=1, source_target_pairs={{0,15},{1,0},{2,1},{3,2},{4,3},{5,4},{6,5},{7,6},{8,7},{9,8},{10,9... | collective-permute-start | bytes 393224 | tf_op jit(solution)/shard_map/ppermute | solution.py:292
  140.7 8.9 %collective-permute-start.15 = (bf16[128,512]{1,0:T(8,128)(2,1)S(1)}, bf16[128,512]{1,0:T(8,128)(2,1)S(1)}, u32[]{:S(2)}, u32[]{:S(2)}) collective-permute-start(bf16[128,512]{1,0:T(8,128)(2,1)S(1)} %get-tuple-element.35), channel_id=1, source_target_pairs={{0,1},{1,2},{2,3},{3,4},{4,5},{5,6},{6,7},{7,8},{8,9},{9,10},{10,1... | collective-permute-start | bytes 393224 | tf_op jit(solution)/shard_map/ppermute | solution.py:289
  150.7 8.5 %collective-permute-start.22 = (bf16[128,512]{1,0:T(8,128)(2,1)S(1)}, bf16[128,512]{1,0:T(8,128)(2,1)S(1)}, u32[]{:S(2)}, u32[]{:S(2)}) collective-permute-start(bf16[128,512]{1,0:T(8,128)(2,1)S(1)} %get-tuple-element.32), channel_id=1, source_target_pairs={{0,15},{1,0},{2,1},{3,2},{4,3},{5,4},{6,5},{7,6},{8,7},{9,8},{10,9... | collective-permute-start | bytes 393224 | tf_op jit(solution)/shard_map/ppermute | solution.py:292
  152.6 8.8 %collective-permute-start.16 = (bf16[128,512]{1,0:T(8,128)(2,1)S(1)}, bf16[128,512]{1,0:T(8,128)(2,1)S(1)}, u32[]{:S(2)}, u32[]{:S(2)}) collective-permute-start(bf16[128,512]{1,0:T(8,128)(2,1)S(1)} %get-tuple-element.33), channel_id=1, source_target_pairs={{0,1},{1,2},{2,3},{3,4},{4,5},{5,6},{6,7},{7,8},{8,9},{9,10},{10,1... | collective-permute-start | bytes 393224 | tf_op jit(solution)/shard_map/ppermute | solution.py:289
  162.4 9.1 %collective-permute-start.23 = (bf16[128,512]{1,0:T(8,128)(2,1)S(1)}, bf16[128,512]{1,0:T(8,128)(2,1)S(1)}, u32[]{:S(2)}, u32[]{:S(2)}) collective-permute-start(bf16[128,512]{1,0:T(8,128)(2,1)S(1)} %get-tuple-element.30), channel_id=1, source_target_pairs={{0,15},{1,0},{2,1},{3,2},{4,3},{5,4},{6,5},{7,6},{8,7},{9,8},{10,9... | collective-permute-start | bytes 393224 | tf_op jit(solution)/shard_map/ppermute | solution.py:292
  165.5 11.5 %collective-permute-start.17 = (bf16[128,512]{1,0:T(8,128)(2,1)S(1)}, bf16[128,512]{1,0:T(8,128)(2,1)S(1)}, u32[]{:S(2)}, u32[]{:S(2)}) collective-permute-start(bf16[128,512]{1,0:T(8,128)(2,1)S(1)} %get-tuple-element.31), channel_id=1, source_target_pairs={{0,1},{1,2},{2,3},{3,4},{4,5},{5,6},{6,7},{7,8},{8,9},{9,10},{10,1... | collective-permute-start | bytes 393224 | tf_op jit(solution)/shard_map/ppermute | solution.py:289
  179.0 9.1 %collective-permute-start.18 = (bf16[128,512]{1,0:T(8,128)(2,1)S(1)}, bf16[128,512]{1,0:T(8,128)(2,1)S(1)}, u32[]{:S(2)}, u32[]{:S(2)}) collective-permute-start(bf16[128,512]{1,0:T(8,128)(2,1)S(1)} %get-tuple-element.29), channel_id=1, source_target_pairs={{0,1},{1,2},{2,3},{3,4},{4,5},{5,6},{6,7},{7,8},{8,9},{9,10},{10,1... | collective-permute-start | bytes 393224 | tf_op jit(solution)/shard_map/ppermute | solution.py:289
  188.1 16.6 %collective-permute-start.25 = (bf16[128,512]{1,0:T(8,128)(2,1)S(1)}, bf16[128,512]{1,0:T(8,128)(2,1)S(1)}, u32[]{:S(2)}, u32[]{:S(2)}) collective-permute-start(bf16[128,512]{1,0:T(8,128)(2,1)S(1)} %get-tuple-element.26), channel_id=1, source_target_pairs={{0,15},{1,0},{2,1},{3,2},{4,3},{5,4},{6,5},{7,6},{8,7},{9,8},{10,9... | collective-permute-start | bytes 393224 | tf_op jit(solution)/shard_map/ppermute | solution.py:292
  190.8 14.0 %collective-permute-start.19 = (bf16[128,512]{1,0:T(8,128)(2,1)S(1)}, bf16[128,512]{1,0:T(8,128)(2,1)S(1)}, u32[]{:S(2)}, u32[]{:S(2)}) collective-permute-start(bf16[128,512]{1,0:T(8,128)(2,1)S(1)} %get-tuple-element.27), channel_id=1, source_target_pairs={{0,1},{1,2},{2,3},{3,4},{4,5},{5,6},{6,7},{7,8},{8,9},{9,10},{10,1... | collective-permute-start | bytes 393224 | tf_op jit(solution)/shard_map/ppermute | solution.py:289
  194.0 24.4 %all-to-all-start.1 = ((bf16[32,8,1280]{2,1,0:T(8,128)(2,1)}), bf16[32,8,1280]{2,1,0:T(8,128)(2,1)S(1)}, u32[]{:S(2)}, u32[]{:S(2)}) async-start(bf16[32,8,1280]{2,1,0:T(8,128)(2,1)} %bitcast.5), calls=%async_computation.1 | async-start | bytes 1310720 | tf_op jit(solution)/shard_map/all_to_all | solution.py:297
  216.4 10.8 %collective-permute-start.27 = (bf16[128,512]{1,0:T(8,128)(2,1)S(1)}, bf16[128,512]{1,0:T(8,128)(2,1)S(1)}, u32[]{:S(2)}, u32[]{:S(2)}) collective-permute-start(bf16[128,512]{1,0:T(8,128)(2,1)S(1)} %get-tuple-element.20), channel_id=1, source_target_pairs={{0,1},{1,2},{2,3},{3,4},{4,5},{5,6},{6,7},{7,8},{8,9},{9,10},{10,1... | collective-permute-start | bytes 393224 | tf_op jit(solution)/shard_map/ppermute | solution.py:289
  (30 other events, 745.8 us)
Sparse Core Ops, SparseCore 0:
  10.7 80.0 all-gather.1
  121.2 71.2 reduce-scatter.1

commit v2 on v1

v2 whole, which is shorter than its diff:
```python
import jax
import jax.numpy as jnp
from jax import lax
from jax.experimental import pallas as pl
from jax.experimental.pallas import tpu as pltpu
from jax.sharding import Mesh, PartitionSpec as P

HEAD_DIM = 128
GROUP = 4
CAP = 5
OWNERS = 32
PAIR = 2
ROWS = 2048
SHARD = 128
TOK = 128
SLAB = OWNERS * 8
RECV = PAIR * SLAB
QUERIES = PAIR * OWNERS * CAP * GROUP
BLOCK = 256
SCALE = HEAD_DIM ** -0.5
EXP2_SCALE = SCALE * 1.4426950408889634
VMEM_LIMIT = 56 * 1024 * 1024

f32 = jnp.float32
bf16 = jnp.bfloat16


def dot(a, b):
    return jnp.dot(a, b, preferred_element_type=f32)


def iota(shape, dim):
    return lax.broadcasted_iota(jnp.int32, shape, dim)


def one_hot(mask):
    return jnp.where(mask, 1.0, 0.0).astype(bf16)


def bases(owner, rank):
    out = []
    for first in (0, 2):
        here = (rank >= first) & (rank < first + 2)
        out.append(jnp.where(here, owner * 8 + (rank - first) * 4, -64))
    out.append(jnp.where(rank == 4, owner * 8, -64))
    return out


def pack_kernel(row_ref, col_ref, q_ref, c_ref, out_ref):
    row = row_ref[...]
    same = jnp.broadcast_to(col_ref[...], (TOK, TOK)) == jnp.broadcast_to(row, (TOK, TOK))
    before = iota((TOK, TOK), 0) < iota((TOK, TOK), 1)
    rank = jnp.sum(jnp.where(same & before, 1, 0), axis=0, keepdims=True)
    base = bases(row, rank)
    slab_row = iota((SLAB, TOK), 0)

    def place(first, count):
        wide = jnp.broadcast_to(first, (SLAB, TOK))
        return jnp.concatenate([one_hot(slab_row == wide + j) for j in range(count)], axis=1)

    def head(ref, h):
        return ref[:, h * HEAD_DIM:(h + 1) * HEAD_DIM]

    full = jnp.concatenate(
        [jnp.concatenate([head(r, 4 * k + j) for r in (q_ref, c_ref) for k in range(4)], axis=1) for j in range(4)],
        axis=0,
    )
    for g in range(2):
        slab = dot(place(base[g], 4), full).astype(bf16)
        for p in range(2):
            rows = slice(p * SLAB, (p + 1) * SLAB)
            out_ref[rows, g * 256:(g + 1) * 256] = slab[:, p * 256:(p + 1) * 256]
            out_ref[rows, 640 + g * 256:640 + (g + 1) * 256] = slab[:, 512 + p * 256:512 + (p + 1) * 256]
    last = jnp.concatenate(
        [
            jnp.concatenate([head(r, 4 * (2 * p + kk) + j) for r in (q_ref, c_ref) for p in range(2)], axis=1)
            for kk in range(2)
            for j in range(4)
        ],
        axis=0,
    )
    slab = dot(place(base[2], 8), last).astype(bf16)
    for p in range(2):
        rows = slice(p * SLAB, (p + 1) * SLAB)
        out_ref[rows, 512:640] = slab[:, p * 128:(p + 1) * 128]
        out_ref[rows, 1152:1280] = slab[:, 256 + p * 128:256 + (p + 1) * 128]


def unpack_kernel(row_ref, col_ref, in_ref, out_ref):
    col = col_ref[...]
    same = jnp.broadcast_to(col, (TOK, TOK)) == jnp.broadcast_to(row_ref[...], (TOK, TOK))
    before = iota((TOK, TOK), 1) < iota((TOK, TOK), 0)
    rank = jnp.sum(jnp.where(same & before, 1, 0), axis=1, keepdims=True)
    base = bases(col, rank)
    slab_col = iota((TOK, SLAB), 1)

    def pick(first, count):
        wide = jnp.broadcast_to(first, (TOK, SLAB))
        return jnp.concatenate([one_hot(slab_col == wide + j) for j in range(count)], axis=0)

    total = None
    for g in range(2):
        slab = jnp.concatenate([in_ref[0:SLAB, g * 256:(g + 1) * 256], in_ref[SLAB:RECV, g * 256:(g + 1) * 256]], axis=1)
        part = dot(pick(base[g], 4), slab)
        total = part if total is None else total + part
    last = dot(pick(base[2], 8), jnp.concatenate([in_ref[0:SLAB, 512:640], in_ref[SLAB:RECV, 512:640]], axis=1))
    for k in range(4):
        for j in range(4):
            h = 4 * k + j
            first = ((k % 2) * 4 + j) * TOK
            value = total[j * TOK:(j + 1) * TOK, k * 128:(k + 1) * 128]
            value = value + last[first:first + TOK, (k // 2) * 128:(k // 2 + 1) * 128]
            out_ref[:, h * HEAD_DIM:(h + 1) * HEAD_DIM] = value.astype(bf16)


def attend_kernel(recv_ref, kv_ref, out_ref, grad_ref, q_s, c_s, qt_s, ct_s, s_s, w_s, acc_s):
    half_row = iota((RECV // 2, RECV), 0)
    half_col = iota((RECV // 2, RECV), 1)
    back_row = iota((RECV, RECV // 2), 0)
    back_col = iota((RECV, RECV // 2), 1)
    lanes = [(slice(kk * 128, (kk + 1) * 128), slice(256 + kk * 128, 256 + (kk + 1) * 128)) for kk in range(2)]

    def rows_of(i):
        return pl.ds(pl.multiple_of(i * BLOCK, BLOCK), BLOCK)

    def load(kk):
        take = one_hot(half_col == (half_row // 4) * 8 + kk * 4 + half_row % 4)
        for ref, first in ((q_s, 0), (c_s, 640)):
            ref[kk, 0:RECV, :] = recv_ref[:, first + kk * 128:first + (kk + 1) * 128]
            ref[kk, RECV:2 * RECV, :] = recv_ref[:, first + 256 + kk * 128:first + 256 + (kk + 1) * 128]
            ref[kk, 2 * RECV:QUERIES, :] = dot(take, recv_ref[:, first + 512:first + 640]).astype(bf16)
        qt_s[kk] = q_s[kk].astype(f32).T.astype(bf16)
        acc_s[kk] = jnp.zeros((HEAD_DIM, QUERIES), f32)

    def score(kk, i, top):
        s = dot(kv_ref[rows_of(i), lanes[kk][0]], qt_s[kk])
        s_s[kk, rows_of(i), :] = s
        return jnp.maximum(top, jnp.max(s, axis=0, keepdims=True))

    def weigh(kk, i, top, total):
        w = jnp.exp2(s_s[kk, rows_of(i), :] * EXP2_SCALE - top)
        wb = w.astype(bf16)
        w_s[kk, rows_of(i), :] = wb
        vt = kv_ref[rows_of(i), lanes[kk][1]].astype(f32).T.astype(bf16)
        acc_s[kk] += dot(vt, wb)
        return total + jnp.sum(w, axis=0, keepdims=True)

    def finish(kk, total):
        inverse = 1.0 / total
        out_t = acc_s[kk] * inverse
        ct = (c_s[kk].astype(f32).T * inverse).astype(bf16)
        ct_s[kk] = ct
        c_s[kk] = ct.astype(f32).T.astype(bf16)
        out = out_t.T.astype(bf16)
        out_ref[:, kk * 128:(kk + 1) * 128] = out[0:RECV, :]
        out_ref[:, 256 + kk * 128:256 + (kk + 1) * 128] = out[RECV:2 * RECV, :]
        give = one_hot(back_row == (back_col // 4) * 8 + kk * 4 + back_col % 4)
        return jnp.sum(ct.astype(f32) * out_t, axis=0, keepdims=True), dot(give, out[2 * RECV:QUERIES, :])

    def grads(kk, i, delta):
        key, val = lanes[kk]
        wb = w_s[kk, rows_of(i), :]
        prob_grad = dot(kv_ref[rows_of(i), val], ct_s[kk])
        ds = (wb.astype(f32) * (prob_grad - delta)).astype(bf16)
        grad_ref[rows_of(i), val] = dot(wb, c_s[kk]).astype(bf16)
        grad_ref[rows_of(i), key] = (dot(ds, q_s[kk]) * SCALE).astype(bf16)

    steps = ROWS // BLOCK
    lowest = jnp.full((1, QUERIES), -jnp.inf, f32)
    zero = jnp.zeros((1, QUERIES), f32)

    load(0)
    top0 = lax.fori_loop(0, steps, lambda i, top: score(0, i, top), lowest) * EXP2_SCALE
    load(1)

    def second(i, carry):
        top, total = carry
        return score(1, i, top), weigh(0, i, top0, total)

    top1, total0 = lax.fori_loop(0, steps, second, (lowest, zero))
    top1 = top1 * EXP2_SCALE
    delta0, tail0 = finish(0, total0)

    def third(i, total):
        grads(0, i, delta0)
        return weigh(1, i, top1, total)

    total1 = lax.fori_loop(0, steps, third, zero)
    delta1, tail1 = finish(1, total1)
    out_ref[:, 512:640] = (tail0 + tail1).astype(bf16)

    def fourth(i, carry):
        grads(1, i, delta1)
        return carry

    lax.fori_loop(0, steps, fourth, 0)


def split_kernel(side_ref, in_ref, keep_ref, send_ref):
    def copy(to_ref, half):
        to_ref[:, 0:256] = in_ref[:, half * 256:(half + 1) * 256]
        to_ref[:, 256:512] = in_ref[:, 512 + half * 256:512 + (half + 1) * 256]

    for side in range(2):

        @pl.when(side_ref[0] == side)
        def _():
            copy(keep_ref, side)
            copy(send_ref, 1 - side)


def join_kernel(side_ref, own_ref, other_ref, out_ref):
    def copy(ref, half):
        out_ref[:, half * 256:(half + 1) * 256] = ref[0:SHARD, 0:256].astype(f32)
        out_ref[:, 512 + half * 256:512 + (half + 1) * 256] = ref[0:SHARD, 256:512].astype(f32)

    for side in range(2):

        @pl.when(side_ref[0] == side)
        def _():
            copy(own_ref, side)
            copy(other_ref, 1 - side)


def vmem(count):
    return [pl.BlockSpec(memory_space=pltpu.VMEM)] * count


SMEM = pl.BlockSpec(memory_space=pltpu.SMEM)
WORK = [
    pltpu.VMEM((2, QUERIES, HEAD_DIM), bf16),
    pltpu.VMEM((2, QUERIES, HEAD_DIM), bf16),
    pltpu.VMEM((2, HEAD_DIM, QUERIES), bf16),
    pltpu.VMEM((2, HEAD_DIM, QUERIES), bf16),
    pltpu.VMEM((2, ROWS, QUERIES), f32),
    pltpu.VMEM((2, ROWS, QUERIES), bf16),
    pltpu.VMEM((2, HEAD_DIM, QUERIES), f32),
]
PARAMS = pltpu.CompilerParams(vmem_limit_bytes=VMEM_LIMIT)
ATTEND_COST = pl.CostEstimate(
    flops=2 * 5 * QUERIES * ROWS * HEAD_DIM * 2, bytes_accessed=6 * 1024 * 1024, transcendentals=2 * QUERIES * ROWS
)
SMALL_COST = pl.CostEstimate(flops=2 * 1024 * 1024 * 1024, bytes_accessed=3 * 1024 * 1024, transcendentals=0)


def local(queries, cotangent, corpus_of, cartridge):
    side = lax.axis_index("zl").astype(jnp.int32).reshape(1)
    swap = [(0, 1), (1, 0)]
    keep, send = pl.pallas_call(
        split_kernel,
        out_shape=(jax.ShapeDtypeStruct((SHARD, 512), bf16), jax.ShapeDtypeStruct((SHARD, 512), bf16)),
        in_specs=[SMEM] + vmem(1),
        out_specs=tuple(vmem(2)),
        compiler_params=PARAMS,
        name="split",
    )(side, cartridge[0])
    taken = lax.ppermute(send, "zl", swap)
    gathered = lax.all_gather(jnp.concatenate([keep, taken], axis=0), "zh", axis=0, tiled=True)

    col = corpus_of.astype(jnp.int32)
    row = col.reshape(1, TOK)
    packed = pl.pallas_call(
        pack_kernel,
        out_shape=jax.ShapeDtypeStruct((RECV, 1280), bf16),
        in_specs=vmem(4),
        out_specs=vmem(1)[0],
        compiler_params=PARAMS,
        cost_estimate=SMALL_COST,
        name="pack",
    )(row, col, queries, cotangent)
    packed, taken = lax.optimization_barrier((packed, taken))
    recv = lax.all_to_all(packed, ("zl", "corpus"), split_axis=0, concat_axis=0, tiled=True)

    out, grads = pl.pallas_call(
        attend_kernel,
        out_shape=(jax.ShapeDtypeStruct((RECV, 640), bf16), jax.ShapeDtypeStruct((ROWS, 512), bf16)),
        in_specs=vmem(2),
        out_specs=tuple(vmem(2)),
        scratch_shapes=WORK,
        compiler_params=PARAMS,
        cost_estimate=ATTEND_COST,
        name="attend",
    )(recv, gathered)

    summed = lax.psum_scatter(grads, "zh", scatter_dimension=0, tiled=True)
    other = lax.ppermute(summed[SHARD:], "zl", swap)
    grad = pl.pallas_call(
        join_kernel,
        out_shape=jax.ShapeDtypeStruct((SHARD, 1024), f32),
        in_specs=[SMEM] + vmem(2),
        out_specs=vmem(1)[0],
        compiler_params=PARAMS,
        name="join",
    )(side, summed, other)

    replies = lax.all_to_all(out, ("zl", "corpus"), split_axis=0, concat_axis=0, tiled=True)
    attended = pl.pallas_call(
        unpack_kernel,
        out_shape=jax.ShapeDtypeStruct((TOK, 2048), bf16),
        in_specs=vmem(3),
        out_specs=vmem(1)[0],
        compiler_params=PARAMS,
        cost_estimate=SMALL_COST,
        name="unpack",
    )(row, col, replies)
    return attended, grad[None]


def solution(mesh):
    corpus, conv = mesh.devices.shape
    pairs = Mesh(mesh.devices.reshape(corpus, conv // PAIR, PAIR), ("corpus", "zh", "zl"))
    tokens = P(("corpus", "zh", "zl"), None)
    rows = P("corpus", ("zh", "zl"), None)
    return jax.shard_map(
        local,
        mesh=pairs,
        in_specs=(tokens, tokens, tokens, rows),
        out_specs=(tokens, rows),
        check_vma=False,
    )
```

time: 244 us -> 204 us (0.84)
  starting transfers between devices: 121 us -> 24.7 us
  waiting for transfers between devices: 59.1 us -> 123 us
  Pallas kernels: 39.2 us -> 35 us
  other arithmetic: 3.94 us -> 0.72 us
    ppermute x30 -> x2, starting transfers between devices: 101 us -> 6.79 us  [the longest x1 3.81 us: local(): taken = lax.ppermute(send, 'zl', swap)]
    all_gather x1, waiting for transfers between devices: 0.02 us -> 69.7 us  [local(): lax.all_gather(jnp.concatenate([keep, taken], axis=0), 'zh', axis=0, tile...]
    ppermute x30 -> x2, waiting for transfers between devices: 59 us -> 0.23 us  [the longest x1 0.23 us: local(): other = lax.ppermute(summed[SHARD:], 'zl', swap)]
    reduce_scatter x1, waiting for transfers between devices: 0.02 us -> 52.9 us  [local(): summed = lax.psum_scatter(grads, 'zh', scatter_dimension=0, tiled=True)]
    pallas_call x3 -> x4, Pallas kernels: 36.3 us -> 32.2 us  [the longest x1 25.3 us: local(): pl.pallas_call(attend_kernel, out_shape=(jax.ShapeDtypeStruct((RECV, 640)...]
    all_to_all x2, starting transfers between devices: 20.2 us -> 17.8 us  [the longest x1 9.36 us: local(): lax.all_to_all(out, ('zl', 'corpus'), split_axis=0, concat_axis=0, tiled=...]
  transfers between devices with their start and end apart: 34 -> 6, of which waited for: 24 -> 3; matrix products, arithmetic and copies ran while one was open for 2% -> 1% of each run, Pallas kernels for 16% -> 3%
where the time goes in v2:
time: 204 us; the launch traced here: 202 us
  waiting for transfers between devices  123 us (60%)
  Pallas kernels  35 us (17%)
  starting transfers between devices  24.7 us (12%)
  between operations  14.1 us (7%)
  local copies, waits for them, and re-layouts  4.89 us (2%)
    all_gather x1, waiting for transfers between devices, local(): lax.all_gather(jnp.concatenate([keep, taken], axis=0), 'zh', axis=0, tile...  69.7 us
    reduce_scatter x1, waiting for transfers between devices, local(): summed = lax.psum_scatter(grads, 'zh', scatter_dimension=0, tiled=True)  52.9 us
    pallas_call x1, Pallas kernels, local(): pl.pallas_call(attend_kernel, out_shape=(jax.ShapeDtypeStruct((RECV, 640)...  25.3 us
    all_to_all x1, starting transfers between devices, local(): lax.all_to_all(out, ('zl', 'corpus'), split_axis=0, concat_axis=0, tiled=...  9.36 us
    all_to_all x1, starting transfers between devices, local(): lax.all_to_all(packed, ('zl', 'corpus'), split_axis=0, concat_axis=0, til...  8.43 us
  transfers between devices with their start and end apart: 6, of which 3 were waited for; matrix products, arithmetic and copies ran while one was open for 1% of the time, Pallas kernels for 3%

profile of v2, /device:TPU:6, one launch (start us, length us, event | category | flops | bytes accessed | tf_op | source)
XLA Modules:
  0.0 202.3 jit_solution(7242483149513420469)
XLA Ops:
  7.2 1.7 split.1
  8.8 3.8 %collective-permute-start = (bf16[128,512]{1,0:T(8,128)(2,1)}, bf16[128,512]{1,0:T(8,128)(2,1)S(1)}, u32[]{:S(2)}, u32[]{:S(2)}) collective-permute-start(bf16[128,512]{1,0:T(8,128)(2,1)} %get-tuple-element.7), channel_id=1, source_target_pairs={{0,1},{1,0},{2,3},{3,2},{4,5},{5,4},{6,7},{7,6},{8,9},{9,8},{10,11... | collective-permute-start | bytes 393224 | tf_op jit(solution)/shard_map/ppermute | solution.py:257
  12.7 1.4 copy.7.col_ref
  14.0 3.4 %pack.1 = bf16[512,1280]{1,0:T(8,128)(2,1)} custom-call(s32[1,128]{1,0:T(1,128)} %bitcast.13, s32[128,1]{1,0:T(8,128)} %copy.7.col_ref, bf16[128,2048]{1,0:T(8,128)(2,1)} %q_ref.1, bf16[128,2048]{1,0:T(8,128)(2,1)} %c_ref.1), custom_call_target="tpu_custom_call" | custom-call | flops 2147483648 | bytes 3145728 | tf_op jit(solution)/shard_map/pack/pallas_call | solution.py:262
  17.4 0.0 collective-permute-done
  17.4 8.4 %all-to-all-start = ((bf16[64,8,1280]{2,1,0:T(8,128)(2,1)}), bf16[64,8,1280]{2,1,0:T(8,128)(2,1)S(1)}, u32[]{:S(2)}, u32[]{:S(2)}) async-start(bf16[64,8,1280]{2,1,0:T(8,128)(2,1)} %bitcast.9), calls=%async_computation | async-start | bytes 2621440 | tf_op jit(solution)/shard_map/all_to_all | solution.py:272
  25.9 0.0 all-gather.2.cloned.1.call-start
  25.9 0.7 pad_maximum_fusion
  26.7 0.0 all-gather.2.cloned.1.call-update
  26.7 0.0 reduce-scatter.2.cloned.1.call-start
  26.7 69.7 %all-gather.2.cloned.1.call-done.kv_ref = bf16[2048,512]{1,0:T(8,128)(2,1)} async-done(((bf16[256,512]{1,0:T(8,128)(2,1)}), bf16[2048,512]{1,0:T(8,128)(2,1)}) %all-gather.2.cloned.1.call-update) | async-done | bytes 2097168 | tf_op jit(solution)/shard_map/all_gather | solution.py:258
  96.5 1.1 copy-done
  97.6 25.3 %attend.1 = (bf16[512,640]{1,0:T(8,128)(2,1)}, bf16[2048,512]{1,0:T(8,128)(2,1)}) custom-call(bf16[512,1280]{1,0:T(8,128)(2,1)} %bitcast.8, bf16[2048,512]{1,0:T(8,128)(2,1)} %all-gather.2.cloned.1.call-done.kv_ref), custom_call_target="tpu_custom_call" | custom-call | flops 6710886400 | bytes 6291456 | tf_op jit(solution)/shard_map/attend/pallas_call | solution.py:274
  122.9 0.0 reduce-scatter.2.cloned.1.call-update
  122.9 9.4 %all-to-all-start.1 = ((bf16[64,8,640]{2,1,0:T(8,128)(2,1)}), bf16[64,8,640]{2,1,0:T(8,128)(2,1)S(1)}, u32[]{:S(2)}, u32[]{:S(2)}) async-start(bf16[64,8,640]{2,1,0:T(8,128)(2,1)} %bitcast.5), calls=%async_computation.1 | async-start | bytes 1310720 | tf_op jit(solution)/shard_map/all_to_all | solution.py:296
  132.3 52.9 %reduce-scatter.2.cloned.1.call-done.own_ref = bf16[256,512]{1,0:T(8,128)(2,1)} async-done(((bf16[2048,512]{1,0:T(8,128)(2,1)}), bf16[256,512]{1,0:T(8,128)(2,1)}) %reduce-scatter.2.cloned.1.call-update) | async-done | bytes 262160 | tf_op jit(solution)/shard_map/reduce_scatter | solution.py:285
  185.2 0.9 slice.4
  186.1 3.0 %collective-permute-start.1 = (bf16[128,512]{1,0:T(8,128)(2,1)S(1)}, bf16[128,512]{1,0:T(8,128)(2,1)S(1)}, u32[]{:S(2)}, u32[]{:S(2)}) collective-permute-start(bf16[128,512]{1,0:T(8,128)(2,1)S(1)} %slice.4), channel_id=1, source_target_pairs={{0,1},{1,0},{2,3},{3,2},{4,5},{5,4},{6,7},{7,6},{8,9},{9,8},{10,11... | collective-permute-start | bytes 393224 | tf_op jit(solution)/shard_map/ppermute | solution.py:286
  189.1 0.0 all-to-all-done.1
  189.1 0.8 copy-done.1
  190.0 2.8 %unpack.1 = bf16[128,2048]{1,0:T(8,128)(2,1)} custom-call(s32[1,128]{1,0:T(1,128)} %bitcast.14, s32[128,1]{1,0:T(8,128)} %copy.7.col_ref, bf16[512,640]{1,0:T(8,128)(2,1)} %bitcast.10), custom_call_target="tpu_custom_call" | custom-call | flops 2147483648 | bytes 3145728 | tf_op jit(solution)/shard_map/unpack/pallas_call | solution.py:297
  192.8 0.2 collective-permute-done.1.other_ref
  193.0 0.7 copy-done.2
  193.7 1.8 join.1
  (6 shorter events, 0.0 us)
Async XLA Ops:
  8.8 8.6 %collective-permute-start = (bf16[128,512]{1,0:T(8,128)(2,1)}, bf16[128,512]{1,0:T(8,128)(2,1)S(1)}, u32[]{:S(2)}, u32[]{:S(2)}) collective-permute-start(bf16[128,512]{1,0:T(8,128)(2,1)} %get-tuple-element.7), channel_id=1, source_target_pairs={{0,1},{1,0},{2,3},{3,2},{4,5},{5,4},{6,7},{7,6},{8,9},{9,8},{10,11... | collective-permute-start | bytes 393224 | tf_op jit(solution)/shard_map/ppermute | solution.py:257
  17.4 8.5 %copy-start.3 = (bf16[128,512]{1,0:T(8,128)(2,1)S(1)}, bf16[128,512]{1,0:T(8,128)(2,1)}, u32[]{:S(2)}) copy-start(bf16[128,512]{1,0:T(8,128)(2,1)} %get-tuple-element.9) | copy-start | bytes 393220
  17.4 79.0 %all-to-all-start = ((bf16[64,8,1280]{2,1,0:T(8,128)(2,1)}), bf16[64,8,1280]{2,1,0:T(8,128)(2,1)S(1)}, u32[]{:S(2)}, u32[]{:S(2)}) async-start(bf16[64,8,1280]{2,1,0:T(8,128)(2,1)} %bitcast.9), calls=%async_computation | async-start | bytes 2621440 | tf_op jit(solution)/shard_map/all_to_all | solution.py:272
  25.9 70.6 %all-gather.2.cloned.1.call-start = ((), (), s32[]{:S(2)}) async-start(), calls=%async_computation.3 | async-start | bytes 2359296 | tf_op jit(solution)/shard_map/all_gather | solution.py:258
  26.7 158.5 %reduce-scatter.2.cloned.1.call-start = ((), (), s32[]{:S(2)}) async-start(), calls=%async_computation.4 | async-start | bytes 2359296 | tf_op jit(solution)/shard_map/reduce_scatter | solution.py:285
  96.5 1.1 copy-start
  122.9 66.2 %all-to-all-start.1 = ((bf16[64,8,640]{2,1,0:T(8,128)(2,1)}), bf16[64,8,640]{2,1,0:T(8,128)(2,1)S(1)}, u32[]{:S(2)}, u32[]{:S(2)}) async-start(bf16[64,8,640]{2,1,0:T(8,128)(2,1)} %bitcast.5), calls=%async_computation.1 | async-start | bytes 1310720 | tf_op jit(solution)/shard_map/all_to_all | solution.py:296
  186.1 6.9 %collective-permute-start.1 = (bf16[128,512]{1,0:T(8,128)(2,1)S(1)}, bf16[128,512]{1,0:T(8,128)(2,1)S(1)}, u32[]{:S(2)}, u32[]{:S(2)}) collective-permute-start(bf16[128,512]{1,0:T(8,128)(2,1)S(1)} %slice.4), channel_id=1, source_target_pairs={{0,1},{1,0},{2,3},{3,2},{4,5},{5,4},{6,7},{7,6},{8,9},{9,8},{10,11... | collective-permute-start | bytes 393224 | tf_op jit(solution)/shard_map/ppermute | solution.py:286
  189.1 0.8 copy-start.1
  193.0 0.7 copy-start.2
Sparse Core Ops, SparseCore 0:
  29.4 67.0 all-gather.1
  123.0 62.1 reduce-scatter.1

commit v3 on v2

--- a/solution.py
+++ b/solution.py
@@ -16,7 +16,10 @@
 SLAB = OWNERS * 8
 RECV = PAIR * SLAB
 QUERIES = PAIR * OWNERS * CAP * GROUP
-BLOCK = 256
+BLOCK = PAIR * SHARD
+STRIP = 16
+PIECES = BLOCK // STRIP
+WIDE = PIECES * 512
 SCALE = HEAD_DIM ** -0.5
 EXP2_SCALE = SCALE * 1.4426950408889634
 VMEM_LIMIT = 56 * 1024 * 1024
@@ -113,7 +116,7 @@
             out_ref[:, h * HEAD_DIM:(h + 1) * HEAD_DIM] = value.astype(bf16)
 
 
-def attend_kernel(recv_ref, kv_ref, out_ref, grad_ref, q_s, c_s, qt_s, ct_s, s_s, w_s, acc_s):
+def attend_kernel(recv_ref, wide_ref, out_ref, grad_ref, kv_ref, q_s, c_s, qt_s, ct_s, s_s, w_s, acc_s):
     half_row = iota((RECV // 2, RECV), 0)
     half_col = iota((RECV // 2, RECV), 1)
     back_row = iota((RECV, RECV // 2), 0)
@@ -162,13 +165,27 @@
         wb = w_s[kk, rows_of(i), :]
         prob_grad = dot(kv_ref[rows_of(i), val], ct_s[kk])
         ds = (wb.astype(f32) * (prob_grad - delta)).astype(bf16)
-        grad_ref[rows_of(i), val] = dot(wb, c_s[kk]).astype(bf16)
-        grad_ref[rows_of(i), key] = (dot(ds, q_s[kk]) * SCALE).astype(bf16)
+        value_grad = dot(wb, c_s[kk]).astype(bf16)
+        key_grad = (dot(ds, q_s[kk]) * SCALE).astype(bf16)
+        strip = pl.ds(pl.multiple_of(i * STRIP, STRIP), STRIP)
+        for piece in range(PIECES):
+            first = piece * 512 + kk * 128
+            here = slice(piece * STRIP, (piece + 1) * STRIP)
+            grad_ref[strip, first:first + 128] = key_grad[here, :]
+            grad_ref[strip, first + 256:first + 384] = value_grad[here, :]
 
     steps = ROWS // BLOCK
     lowest = jnp.full((1, QUERIES), -jnp.inf, f32)
     zero = jnp.zeros((1, QUERIES), f32)
 
+    def unfold(i, carry):
+        strip = pl.ds(pl.multiple_of(i * STRIP, STRIP), STRIP)
+        for piece in range(PIECES):
+            to = pl.ds(pl.multiple_of(i * BLOCK + piece * STRIP, STRIP), STRIP)
+            kv_ref[to, :] = wide_ref[strip, piece * 512:(piece + 1) * 512]
+        return carry
+
+    lax.fori_loop(0, steps, unfold, 0)
     load(0)
     top0 = lax.fori_loop(0, steps, lambda i, top: score(0, i, top), lowest) * EXP2_SCALE
     load(1)
@@ -198,8 +215,11 @@
 
 def split_kernel(side_ref, in_ref, keep_ref, send_ref):
     def copy(to_ref, half):
-        to_ref[:, 0:256] = in_ref[:, half * 256:(half + 1) * 256]
-        to_ref[:, 256:512] = in_ref[:, 512 + half * 256:512 + (half + 1) * 256]
+        for piece in range(PIECES // 2):
+            rows = slice(piece * STRIP, (piece + 1) * STRIP)
+            first = piece * 512
+            to_ref[:, first:first + 256] = in_ref[rows, half * 256:(half + 1) * 256]
+            to_ref[:, first + 256:first + 512] = in_ref[rows, 512 + half * 256:512 + (half + 1) * 256]
 
     for side in range(2):
 
@@ -211,8 +231,11 @@
 
 def join_kernel(side_ref, own_ref, other_ref, out_ref):
     def copy(ref, half):
-        out_ref[:, half * 256:(half + 1) * 256] = ref[0:SHARD, 0:256].astype(f32)
-        out_ref[:, 512 + half * 256:512 + (half + 1) * 256] = ref[0:SHARD, 256:512].astype(f32)
+        for piece in range(PIECES // 2):
+            rows = slice(piece * STRIP, (piece + 1) * STRIP)
+            first = piece * 512
+            out_ref[rows, half * 256:(half + 1) * 256] = ref[:, first:first + 256].astype(f32)
+            out_ref[rows, 512 + half * 256:512 + (half + 1) * 256] = ref[:, first + 256:first + 512].astype(f32)
 
     for side in range(2):
 
@@ -228,6 +251,7 @@
 
 SMEM = pl.BlockSpec(memory_space=pltpu.SMEM)
 WORK = [
+    pltpu.VMEM((ROWS, 512), bf16),
     pltpu.VMEM((2, QUERIES, HEAD_DIM), bf16),
     pltpu.VMEM((2, QUERIES, HEAD_DIM), bf16),
     pltpu.VMEM((2, HEAD_DIM, QUERIES), bf16),
@@ -248,14 +272,15 @@
     swap = [(0, 1), (1, 0)]
     keep, send = pl.pallas_call(
         split_kernel,
-        out_shape=(jax.ShapeDtypeStruct((SHARD, 512), bf16), jax.ShapeDtypeStruct((SHARD, 512), bf16)),
+        out_shape=(jax.ShapeDtypeStruct((STRIP, WIDE // 2), bf16), jax.ShapeDtypeStruct((STRIP, WIDE // 2), bf16)),
         in_specs=[SMEM] + vmem(1),
         out_specs=tuple(vmem(2)),
         compiler_params=PARAMS,
         name="split",
     )(side, cartridge[0])
     taken = lax.ppermute(send, "zl", swap)
-    gathered = lax.all_gather(jnp.concatenate([keep, taken], axis=0), "zh", axis=0, tiled=True)
+    both = jnp.concatenate([keep, taken], axis=1)
+    gathered = lax.all_gather(both, "zh", axis=0, tiled=True)
 
     col = corpus_of.astype(jnp.int32)
     row = col.reshape(1, TOK)
@@ -268,12 +293,12 @@
         cost_estimate=SMALL_COST,
         name="pack",
     )(row, col, queries, cotangent)
-    packed, taken = lax.optimization_barrier((packed, taken))
+    packed, both = lax.optimization_barrier((packed, both))
     recv = lax.all_to_all(packed, ("zl", "corpus"), split_axis=0, concat_axis=0, tiled=True)
 
     out, grads = pl.pallas_call(
         attend_kernel,
-        out_shape=(jax.ShapeDtypeStruct((RECV, 640), bf16), jax.ShapeDtypeStruct((ROWS, 512), bf16)),
+        out_shape=(jax.ShapeDtypeStruct((RECV, 640), bf16), jax.ShapeDtypeStruct((ROWS // PIECES, WIDE), bf16)),
         in_specs=vmem(2),
         out_specs=tuple(vmem(2)),
         scratch_shapes=WORK,
@@ -283,16 +308,6 @@
     )(recv, gathered)
 
     summed = lax.psum_scatter(grads, "zh", scatter_dimension=0, tiled=True)
-    other = lax.ppermute(summed[SHARD:], "zl", swap)
-    grad = pl.pallas_call(
-        join_kernel,
-        out_shape=jax.ShapeDtypeStruct((SHARD, 1024), f32),
-        in_specs=[SMEM] + vmem(2),
-        out_specs=vmem(1)[0],
-        compiler_params=PARAMS,
-        name="join",
-    )(side, summed, other)
-
     replies = lax.all_to_all(out, ("zl", "corpus"), split_axis=0, concat_axis=0, tiled=True)
     attended = pl.pallas_call(
         unpack_kernel,
@@ -303,6 +318,17 @@
         cost_estimate=SMALL_COST,
         name="unpack",
     )(row, col, replies)
+    summed, attended = lax.optimization_barrier((summed, attended))
+    other = lax.ppermute(summed[:, WIDE // 2:], "zl", swap)
+    grad = pl.pallas_call(
+        join_kernel,
+        out_shape=jax.ShapeDtypeStruct((SHARD, 1024), f32),
+        in_specs=[SMEM] + vmem(2),
+        out_specs=vmem(1)[0],
+        compiler_params=PARAMS,
+        name="join",
+    )(side, summed, other)
+
     return attended, grad[None]
 
 

time: 204 us -> 204 us (level)
  blocking collectives: 0 us -> 31.4 us
  waiting for transfers between devices: 123 us -> 99.1 us
  starting transfers between devices: 24.7 us -> 17.3 us
    all_to_all x0 -> x1, blocking collectives: none -> 31.4 us  [local(): lax.all_to_all(out, ('zl', 'corpus'), split_axis=0, concat_axis=0, tiled=...]
    reduce_scatter x1, waiting for transfers between devices: 52.9 us -> 25.4 us  [local(): summed = lax.psum_scatter(grads, 'zh', scatter_dimension=0, tiled=True)]
    all_to_all x1 -> x0, starting transfers between devices: 9.36 us -> none  [local(): lax.all_to_all(out, ('zl', 'corpus'), split_axis=0, concat_axis=0, tiled=...]
    ppermute x1, waiting for transfers between devices: 0.23 us -> 2.93 us  [local(): other = lax.ppermute(summed[:, WIDE // 2:], 'zl', swap)]
    ppermute x1, starting transfers between devices: 2.98 us -> 5.31 us  [local(): other = lax.ppermute(summed[:, WIDE // 2:], 'zl', swap)]
    unnamed x9 -> x10, local copies, waits for them, and re-layouts: 3.97 us -> 5.11 us
  transfers between devices with their start and end apart: 6 -> 5, of which waited for: 3 -> 3; matrix products, arithmetic and copies ran while one was open for 1% -> 1% of each run, Pallas kernels for 3% -> 3%
where the time goes in v3:
time: 204 us; the launch traced here: 203 us
  waiting for transfers between devices  99.1 us (49%)
  Pallas kernels  35.1 us (17%)
  blocking collectives  31.4 us (15%)
  starting transfers between devices  17.3 us (8%)
  between operations  14.1 us (7%)
  local copies, waits for them, and re-layouts  6.03 us (3%)
    all_gather x1, waiting for transfers between devices, local(): gathered = lax.all_gather(both, 'zh', axis=0, tiled=True)  70 us
    all_to_all x1, blocking collectives, local(): lax.all_to_all(out, ('zl', 'corpus'), split_axis=0, concat_axis=0, tiled=...  31.4 us
    pallas_call x1, Pallas kernels, local(): pl.pallas_call(attend_kernel, out_shape=(jax.ShapeDtypeStruct((RECV, 640)...  25.4 us
    reduce_scatter x1, waiting for transfers between devices, local(): summed = lax.psum_scatter(grads, 'zh', scatter_dimension=0, tiled=True)  25.4 us
    all_to_all x1, starting transfers between devices, local(): lax.all_to_all(packed, ('zl', 'corpus'), split_axis=0, concat_axis=0, til...  8.11 us
    ppermute x1, starting transfers between devices, local(): other = lax.ppermute(summed[:, WIDE // 2:], 'zl', swap)  5.31 us
    unnamed x10, local copies, waits for them, and re-layouts  5.11 us
  transfers between devices with their start and end apart: 5, of which 3 were waited for; matrix products, arithmetic and copies ran while one was open for 1% of the time, Pallas kernels for 3%

profile of v3, /device:TPU:6, one launch (start us, length us, event | category | flops | bytes accessed | tf_op | source)
XLA Modules:
  0.0 203.0 jit_solution(3261777071383884662)
XLA Ops:
  7.2 1.7 split.1
  8.8 3.8 %collective-permute-start = (bf16[16,4096]{1,0:T(8,128)(2,1)}, bf16[16,4096]{1,0:T(8,128)(2,1)S(1)}, u32[]{:S(2)}, u32[]{:S(2)}) collective-permute-start(bf16[16,4096]{1,0:T(8,128)(2,1)} %get-tuple-element.10), channel_id=1, source_target_pairs={{0,1},{1,0},{2,3},{3,2},{4,5},{5,4},{6,7},{7,6},{8,9},{9,8},{10,11... | collective-permute-start | bytes 393224 | tf_op jit(solution)/shard_map/ppermute | solution.py:281
  12.7 1.4 copy.6.col_ref
  14.0 0.9 constant_dynamic-update-slice_fusion.1
  15.0 3.4 %pack.1 = bf16[512,1280]{1,0:T(8,128)(2,1)} custom-call(s32[1,128]{1,0:T(1,128)} %bitcast.14, s32[128,1]{1,0:T(8,128)} %copy.6.col_ref, bf16[128,2048]{1,0:T(8,128)(2,1)} %q_ref.1, bf16[128,2048]{1,0:T(8,128)(2,1)} %c_ref.1), custom_call_target="tpu_custom_call" | custom-call | flops 2147483648 | bytes 3145728 | tf_op jit(solution)/shard_map/pack/pallas_call | solution.py:287
  18.4 0.0 copy-start.2
  18.4 8.1 %all-to-all-start = ((bf16[64,8,1280]{2,1,0:T(8,128)(2,1)}), bf16[64,8,1280]{2,1,0:T(8,128)(2,1)S(1)}, u32[]{:S(2)}, u32[]{:S(2)}) async-start(bf16[64,8,1280]{2,1,0:T(8,128)(2,1)} %bitcast.8), calls=%async_computation | async-start | bytes 2621440 | tf_op jit(solution)/shard_map/all_to_all | solution.py:297
  26.5 0.0 all-gather.2.cloned.1.call-start
  26.6 0.7 all-gather.2.cloned.1.call-update
  27.2 0.0 reduce-scatter.2.cloned.1.call-start
  27.3 70.0 %all-gather.2.cloned.1.call-done.wide_ref = bf16[128,8192]{1,0:T(8,128)(2,1)} async-done(((bf16[16,8192]{1,0:T(8,128)(2,1)}), bf16[128,8192]{1,0:T(8,128)(2,1)}) %all-gather.2.cloned.1.call-update) | async-done | bytes 2097168 | tf_op jit(solution)/shard_map/all_gather | solution.py:283
  97.3 0.0 all-to-all-done
  97.3 1.1 copy-done
  98.4 25.4 %attend.1 = (bf16[512,640]{1,0:T(8,128)(2,1)}, bf16[128,8192]{1,0:T(8,128)(2,1)}) custom-call(bf16[512,1280]{1,0:T(8,128)(2,1)} %bitcast.9, bf16[128,8192]{1,0:T(8,128)(2,1)} %all-gather.2.cloned.1.call-done.wide_ref), custom_call_target="tpu_custom_call" | custom-call | flops 6710886400 | bytes 6291456 | tf_op jit(solution)/shard_map/attend/pallas_call | solution.py:299
  123.8 0.0 reduce-scatter.2.cloned.1.call-update
  123.9 1.1 copy-done.1
  124.9 31.4 %all_to_all.22 = bf16[64,8,640]{2,1,0:T(8,128)(2,1)} all-to-all(bf16[64,8,640]{2,1,0:T(8,128)(2,1)S(1)} %bitcast.10), channel_id=1, replica_groups=mesh['corpus'=32,'zh'=8,'zl'=2] {'zl','corpus'}, dimensions={0} | all-to-all | bytes 1310720 | tf_op jit(solution)/shard_map/all_to_all | solution.py:311
  156.3 2.8 %unpack.1 = bf16[128,2048]{1,0:T(8,128)(2,1)} custom-call(s32[1,128]{1,0:T(1,128)} %bitcast.15, s32[128,1]{1,0:T(8,128)} %copy.6.col_ref, bf16[512,640]{1,0:T(8,128)(2,1)} %bitcast.11), custom_call_target="tpu_custom_call" | custom-call | flops 2147483648 | bytes 3145728 | tf_op jit(solution)/shard_map/unpack/pallas_call | solution.py:312
  159.1 25.4 %reduce-scatter.2.cloned.1.call-done.own_ref = bf16[16,8192]{1,0:T(8,128)(2,1)} async-done(((bf16[128,8192]{1,0:T(8,128)(2,1)}), bf16[16,8192]{1,0:T(8,128)(2,1)}) %reduce-scatter.2.cloned.1.call-update) | async-done | bytes 262160 | tf_op jit(solution)/shard_map/reduce_scatter | solution.py:310
  184.5 0.9 slice.3
  185.4 5.3 %collective-permute-start.1 = (bf16[16,4096]{1,0:T(8,128)(2,1)S(1)}, bf16[16,4096]{1,0:T(8,128)(2,1)S(1)}, u32[]{:S(2)}, u32[]{:S(2)}) collective-permute-start(bf16[16,4096]{1,0:T(8,128)(2,1)S(1)} %slice.3), channel_id=1, source_target_pairs={{0,1},{1,0},{2,3},{3,2},{4,5},{5,4},{6,7},{7,6},{8,9},{9,8},{10,11... | collective-permute-start | bytes 393224 | tf_op jit(solution)/shard_map/ppermute | solution.py:322
  190.8 2.9 %collective-permute-done.1.other_ref = bf16[16,4096]{1,0:T(8,128)(2,1)S(1)} collective-permute-done((bf16[16,4096]{1,0:T(8,128)(2,1)S(1)}, bf16[16,4096]{1,0:T(8,128)(2,1)S(1)}, u32[]{:S(2)}, u32[]{:S(2)}) %collective-permute-start.1) | collective-permute-done | bytes 131104 | tf_op jit(solution)/shard_map/ppermute | solution.py:322
  193.7 0.6 copy-done.3
  194.3 1.8 join.1
  (6 shorter events, 0.0 us)
Async XLA Ops:
  8.8 9.5 %collective-permute-start = (bf16[16,4096]{1,0:T(8,128)(2,1)}, bf16[16,4096]{1,0:T(8,128)(2,1)S(1)}, u32[]{:S(2)}, u32[]{:S(2)}) collective-permute-start(bf16[16,4096]{1,0:T(8,128)(2,1)} %get-tuple-element.10), channel_id=1, source_target_pairs={{0,1},{1,0},{2,3},{3,2},{4,5},{5,4},{6,7},{7,6},{8,9},{9,8},{10,11... | collective-permute-start | bytes 393224 | tf_op jit(solution)/shard_map/ppermute | solution.py:281
  18.4 8.2 %copy-start.2 = (bf16[16,8192]{1,0:T(8,128)(2,1)}, bf16[16,8192]{1,0:T(8,128)(2,1)S(1)}, u32[]{:S(2)}) copy-start(bf16[16,8192]{1,0:T(8,128)(2,1)S(1)} %constant_dynamic-update-slice_fusion) | copy-start | bytes 786436
  18.4 78.9 %all-to-all-start = ((bf16[64,8,1280]{2,1,0:T(8,128)(2,1)}), bf16[64,8,1280]{2,1,0:T(8,128)(2,1)S(1)}, u32[]{:S(2)}, u32[]{:S(2)}) async-start(bf16[64,8,1280]{2,1,0:T(8,128)(2,1)} %bitcast.8), calls=%async_computation | async-start | bytes 2621440 | tf_op jit(solution)/shard_map/all_to_all | solution.py:297
  26.5 70.8 %all-gather.2.cloned.1.call-start = ((), (), s32[]{:S(2)}) async-start(), calls=%async_computation.3 | async-start | bytes 2359296 | tf_op jit(solution)/shard_map/all_gather | solution.py:283
  27.2 157.3 %reduce-scatter.2.cloned.1.call-start = ((), (), s32[]{:S(2)}) async-start(), calls=%async_computation.4 | async-start | bytes 2359296 | tf_op jit(solution)/shard_map/reduce_scatter | solution.py:310
  97.3 1.1 copy-start
  123.8 1.1 copy-start.1
  185.4 8.2 %collective-permute-start.1 = (bf16[16,4096]{1,0:T(8,128)(2,1)S(1)}, bf16[16,4096]{1,0:T(8,128)(2,1)S(1)}, u32[]{:S(2)}, u32[]{:S(2)}) collective-permute-start(bf16[16,4096]{1,0:T(8,128)(2,1)S(1)} %slice.3), channel_id=1, source_target_pairs={{0,1},{1,0},{2,3},{3,2},{4,5},{5,4},{6,7},{7,6},{8,9},{9,8},{10,11... | collective-permute-start | bytes 393224 | tf_op jit(solution)/shard_map/ppermute | solution.py:322
  193.7 0.7 copy-start.3
Sparse Core Ops, SparseCore 0:
  30.0 67.2 all-gather.1
  124.0 60.4 reduce-scatter.1

commit v4 on v2

--- a/solution.py
+++ b/solution.py
@@ -17,6 +17,7 @@
 RECV = PAIR * SLAB
 QUERIES = PAIR * OWNERS * CAP * GROUP
 BLOCK = 256
+UNROLL = 2
 SCALE = HEAD_DIM ** -0.5
 EXP2_SCALE = SCALE * 1.4426950408889634
 VMEM_LIMIT = 56 * 1024 * 1024
@@ -113,7 +114,16 @@
             out_ref[:, h * HEAD_DIM:(h + 1) * HEAD_DIM] = value.astype(bf16)
 
 
-def attend_kernel(recv_ref, kv_ref, out_ref, grad_ref, q_s, c_s, qt_s, ct_s, s_s, w_s, acc_s):
+def attend_kernel(side_ref, recv_ref, all_ref, out_ref, grad_ref, kv_ref, *refs):
+    q_s, c_s, qt_s, ct_s, s_s, w_s, acc_s = (refs[2 * i:2 * i + 2] for i in range(7))
+    side = side_ref[0]
+    copies = []
+    for part in range(2):
+        lane = pl.multiple_of(512 * part + 256 * side, 256)
+        copies.append(pltpu.make_async_copy(
+            all_ref.at[:, pl.ds(lane, 256)], kv_ref.at[:, pl.ds(256 * part, 256)], refs[14].at[part]
+        ))
+        copies[part].start()
     half_row = iota((RECV // 2, RECV), 0)
     half_col = iota((RECV // 2, RECV), 1)
     back_row = iota((RECV, RECV // 2), 0)
@@ -126,31 +136,31 @@
     def load(kk):
         take = one_hot(half_col == (half_row // 4) * 8 + kk * 4 + half_row % 4)
         for ref, first in ((q_s, 0), (c_s, 640)):
-            ref[kk, 0:RECV, :] = recv_ref[:, first + kk * 128:first + (kk + 1) * 128]
-            ref[kk, RECV:2 * RECV, :] = recv_ref[:, first + 256 + kk * 128:first + 256 + (kk + 1) * 128]
-            ref[kk, 2 * RECV:QUERIES, :] = dot(take, recv_ref[:, first + 512:first + 640]).astype(bf16)
-        qt_s[kk] = q_s[kk].astype(f32).T.astype(bf16)
-        acc_s[kk] = jnp.zeros((HEAD_DIM, QUERIES), f32)
+            ref[kk][0:RECV, :] = recv_ref[:, first + kk * 128:first + (kk + 1) * 128]
+            ref[kk][RECV:2 * RECV, :] = recv_ref[:, first + 256 + kk * 128:first + 256 + (kk + 1) * 128]
+            ref[kk][2 * RECV:QUERIES, :] = dot(take, recv_ref[:, first + 512:first + 640]).astype(bf16)
+        qt_s[kk][...] = q_s[kk][...].astype(f32).T.astype(bf16)
+        acc_s[kk][...] = jnp.zeros((HEAD_DIM, QUERIES), f32)
 
     def score(kk, i, top):
-        s = dot(kv_ref[rows_of(i), lanes[kk][0]], qt_s[kk])
-        s_s[kk, rows_of(i), :] = s
+        s = dot(kv_ref[rows_of(i), lanes[kk][0]], qt_s[kk][...])
+        s_s[kk][rows_of(i), :] = s
         return jnp.maximum(top, jnp.max(s, axis=0, keepdims=True))
 
     def weigh(kk, i, top, total):
-        w = jnp.exp2(s_s[kk, rows_of(i), :] * EXP2_SCALE - top)
+        w = jnp.exp2(s_s[kk][rows_of(i), :] * EXP2_SCALE - top)
         wb = w.astype(bf16)
-        w_s[kk, rows_of(i), :] = wb
+        w_s[kk][rows_of(i), :] = wb
         vt = kv_ref[rows_of(i), lanes[kk][1]].astype(f32).T.astype(bf16)
-        acc_s[kk] += dot(vt, wb)
+        acc_s[kk][...] += dot(vt, wb)
         return total + jnp.sum(w, axis=0, keepdims=True)
 
     def finish(kk, total):
         inverse = 1.0 / total
-        out_t = acc_s[kk] * inverse
-        ct = (c_s[kk].astype(f32).T * inverse).astype(bf16)
-        ct_s[kk] = ct
-        c_s[kk] = ct.astype(f32).T.astype(bf16)
+        out_t = acc_s[kk][...] * inverse
+        ct = (c_s[kk][...].astype(f32).T * inverse).astype(bf16)
+        ct_s[kk][...] = ct
+        c_s[kk][...] = ct.astype(f32).T.astype(bf16)
         out = out_t.T.astype(bf16)
         out_ref[:, kk * 128:(kk + 1) * 128] = out[0:RECV, :]
         out_ref[:, 256 + kk * 128:256 + (kk + 1) * 128] = out[RECV:2 * RECV, :]
@@ -159,25 +169,33 @@
 
     def grads(kk, i, delta):
         key, val = lanes[kk]
-        wb = w_s[kk, rows_of(i), :]
-        prob_grad = dot(kv_ref[rows_of(i), val], ct_s[kk])
+        wb = w_s[kk][rows_of(i), :]
+        prob_grad = dot(kv_ref[rows_of(i), val], ct_s[kk][...])
         ds = (wb.astype(f32) * (prob_grad - delta)).astype(bf16)
-        grad_ref[rows_of(i), val] = dot(wb, c_s[kk]).astype(bf16)
-        grad_ref[rows_of(i), key] = (dot(ds, q_s[kk]) * SCALE).astype(bf16)
+        value_grad = dot(wb, c_s[kk][...]).astype(bf16)
+        key_grad = (dot(ds, q_s[kk][...]) * SCALE).astype(bf16)
+        for sub in range(PAIR):
+            first = i * BLOCK + lax.rem(side + sub, PAIR) * SHARD
+            to = pl.ds(pl.multiple_of(first, SHARD), SHARD)
+            here = slice(sub * SHARD, (sub + 1) * SHARD)
+            grad_ref[to, val] = value_grad[here, :]
+            grad_ref[to, key] = key_grad[here, :]
 
     steps = ROWS // BLOCK
     lowest = jnp.full((1, QUERIES), -jnp.inf, f32)
     zero = jnp.zeros((1, QUERIES), f32)
 
     load(0)
-    top0 = lax.fori_loop(0, steps, lambda i, top: score(0, i, top), lowest) * EXP2_SCALE
     load(1)
+    for copy in copies:
+        copy.wait()
+    top0 = lax.fori_loop(0, steps, lambda i, top: score(0, i, top), lowest, unroll=UNROLL) * EXP2_SCALE
 
     def second(i, carry):
         top, total = carry
         return score(1, i, top), weigh(0, i, top0, total)
 
-    top1, total0 = lax.fori_loop(0, steps, second, (lowest, zero))
+    top1, total0 = lax.fori_loop(0, steps, second, (lowest, zero), unroll=UNROLL)
     top1 = top1 * EXP2_SCALE
     delta0, tail0 = finish(0, total0)
 
@@ -185,7 +203,7 @@
         grads(0, i, delta0)
         return weigh(1, i, top1, total)
 
-    total1 = lax.fori_loop(0, steps, third, zero)
+    total1 = lax.fori_loop(0, steps, third, zero, unroll=UNROLL)
     delta1, tail1 = finish(1, total1)
     out_ref[:, 512:640] = (tail0 + tail1).astype(bf16)
 
@@ -193,20 +211,7 @@
         grads(1, i, delta1)
         return carry
 
-    lax.fori_loop(0, steps, fourth, 0)
-
-
-def split_kernel(side_ref, in_ref, keep_ref, send_ref):
-    def copy(to_ref, half):
-        to_ref[:, 0:256] = in_ref[:, half * 256:(half + 1) * 256]
-        to_ref[:, 256:512] = in_ref[:, 512 + half * 256:512 + (half + 1) * 256]
-
-    for side in range(2):
-
-        @pl.when(side_ref[0] == side)
-        def _():
-            copy(keep_ref, side)
-            copy(send_ref, 1 - side)
+    lax.fori_loop(0, steps, fourth, 0, unroll=UNROLL)
 
 
 def join_kernel(side_ref, own_ref, other_ref, out_ref):
@@ -227,15 +232,18 @@
 
 
 SMEM = pl.BlockSpec(memory_space=pltpu.SMEM)
-WORK = [
-    pltpu.VMEM((2, QUERIES, HEAD_DIM), bf16),
-    pltpu.VMEM((2, QUERIES, HEAD_DIM), bf16),
-    pltpu.VMEM((2, HEAD_DIM, QUERIES), bf16),
-    pltpu.VMEM((2, HEAD_DIM, QUERIES), bf16),
-    pltpu.VMEM((2, ROWS, QUERIES), f32),
-    pltpu.VMEM((2, ROWS, QUERIES), bf16),
-    pltpu.VMEM((2, HEAD_DIM, QUERIES), f32),
-]
+WORK = [pltpu.VMEM((ROWS, 512), bf16)]
+for shape, kind in (
+    ((QUERIES, HEAD_DIM), bf16),
+    ((QUERIES, HEAD_DIM), bf16),
+    ((HEAD_DIM, QUERIES), bf16),
+    ((HEAD_DIM, QUERIES), bf16),
+    ((ROWS, QUERIES), f32),
+    ((ROWS, QUERIES), bf16),
+    ((HEAD_DIM, QUERIES), f32),
+):
+    WORK += [pltpu.VMEM(shape, kind)] * 2
+WORK += [pltpu.SemaphoreType.DMA((2,))]
 PARAMS = pltpu.CompilerParams(vmem_limit_bytes=VMEM_LIMIT)
 ATTEND_COST = pl.CostEstimate(
     flops=2 * 5 * QUERIES * ROWS * HEAD_DIM * 2, bytes_accessed=6 * 1024 * 1024, transcendentals=2 * QUERIES * ROWS
@@ -246,16 +254,7 @@
 def local(queries, cotangent, corpus_of, cartridge):
     side = lax.axis_index("zl").astype(jnp.int32).reshape(1)
     swap = [(0, 1), (1, 0)]
-    keep, send = pl.pallas_call(
-        split_kernel,
-        out_shape=(jax.ShapeDtypeStruct((SHARD, 512), bf16), jax.ShapeDtypeStruct((SHARD, 512), bf16)),
-        in_specs=[SMEM] + vmem(1),
-        out_specs=tuple(vmem(2)),
-        compiler_params=PARAMS,
-        name="split",
-    )(side, cartridge[0])
-    taken = lax.ppermute(send, "zl", swap)
-    gathered = lax.all_gather(jnp.concatenate([keep, taken], axis=0), "zh", axis=0, tiled=True)
+    gathered = lax.all_gather(cartridge, ("zh", "zl"), axis=1, tiled=True)[0]
 
     col = corpus_of.astype(jnp.int32)
     row = col.reshape(1, TOK)
@@ -268,19 +267,18 @@
         cost_estimate=SMALL_COST,
         name="pack",
     )(row, col, queries, cotangent)
-    packed, taken = lax.optimization_barrier((packed, taken))
     recv = lax.all_to_all(packed, ("zl", "corpus"), split_axis=0, concat_axis=0, tiled=True)
 
     out, grads = pl.pallas_call(
         attend_kernel,
         out_shape=(jax.ShapeDtypeStruct((RECV, 640), bf16), jax.ShapeDtypeStruct((ROWS, 512), bf16)),
-        in_specs=vmem(2),
+        in_specs=[SMEM] + vmem(1) + [pl.BlockSpec(memory_space=pl.ANY)],
         out_specs=tuple(vmem(2)),
         scratch_shapes=WORK,
         compiler_params=PARAMS,
         cost_estimate=ATTEND_COST,
         name="attend",
-    )(recv, gathered)
+    )(side, recv, gathered)
 
     summed = lax.psum_scatter(grads, "zh", scatter_dimension=0, tiled=True)
     other = lax.ppermute(summed[SHARD:], "zl", swap)

time: 204 us -> 202 us (level)
  waiting for transfers between devices: 123 us -> 133 us
  Pallas kernels: 35 us -> 30.1 us
  starting transfers between devices: 24.7 us -> 19.9 us
    all_to_all x1, waiting for transfers between devices: 0.01 us -> 24.5 us  [local(): lax.all_to_all(packed, ('zl', 'corpus'), split_axis=0, concat_axis=0, til...]
    all_gather x1, waiting for transfers between devices: 69.7 us -> 52.2 us  [local(): gathered = lax.all_gather(cartridge, ('zh', 'zl'), axis=1, tiled=True)[0]]
    ppermute x1 -> x0, starting transfers between devices: 3.81 us -> none  [local(): taken = lax.ppermute(send, 'zl', swap)]
    pallas_call x1, Pallas kernels: 25.3 us -> 22.1 us  [local(): pl.pallas_call(attend_kernel, out_shape=(jax.ShapeDtypeStruct((RECV, 640)...]
  transfers between devices with their start and end apart: 6 -> 5, of which waited for: 3 -> 4; matrix products, arithmetic and copies ran while one was open for 1% -> 1% of each run, Pallas kernels for 3% -> 3%
where the time goes in v4:
time: 202 us; the launch traced here: 201 us
  waiting for transfers between devices  133 us (66%)
  Pallas kernels  30.1 us (15%)
  starting transfers between devices  19.9 us (10%)
  between operations  14.1 us (7%)
  local copies, waits for them, and re-layouts  3.79 us (2%)
    reduce_scatter x1, waiting for transfers between devices, local(): summed = lax.psum_scatter(grads, 'zh', scatter_dimension=0, tiled=True)  54.3 us
    all_gather x1, waiting for transfers between devices, local(): gathered = lax.all_gather(cartridge, ('zh', 'zl'), axis=1, tiled=True)[0]  52.2 us
    all_to_all x1, waiting for transfers between devices, local(): lax.all_to_all(packed, ('zl', 'corpus'), split_axis=0, concat_axis=0, til...  24.5 us
    pallas_call x1, Pallas kernels, local(): pl.pallas_call(attend_kernel, out_shape=(jax.ShapeDtypeStruct((RECV, 640)...  22.1 us
    all_to_all x1, starting transfers between devices, local(): lax.all_to_all(packed, ('zl', 'corpus'), split_axis=0, concat_axis=0, til...  9.98 us
    all_to_all x1, starting transfers between devices, local(): lax.all_to_all(out, ('zl', 'corpus'), split_axis=0, concat_axis=0, tiled=...  7.94 us
  transfers between devices with their start and end apart: 5, of which 4 were waited for; matrix products, arithmetic and copies ran while one was open for 1% of the time, Pallas kernels for 3%

profile of v4, /device:TPU:6, one launch (start us, length us, event | category | flops | bytes accessed | tf_op | source)
XLA Modules:
  0.0 200.9 jit_solution(3585467532195392915)
XLA Ops:
  7.2 0.0 all-gather.2.cloned.1.call-start
  7.2 0.7 all-gather.2.cloned.1.call-update
  7.9 1.4 copy.7.col_ref
  9.3 3.4 %pack.1 = bf16[512,1280]{1,0:T(8,128)(2,1)} custom-call(s32[1,128]{1,0:T(1,128)} %bitcast.12, s32[128,1]{1,0:T(8,128)} %copy.7.col_ref, bf16[128,2048]{1,0:T(8,128)(2,1)} %q_ref.1, bf16[128,2048]{1,0:T(8,128)(2,1)} %c_ref.1), custom_call_target="tpu_custom_call" | custom-call | flops 2147483648 | bytes 3145728 | tf_op jit(solution)/shard_map/pack/pallas_call | solution.py:261
  12.7 10.0 %all-to-all-start = ((bf16[64,8,1280]{2,1,0:T(8,128)(2,1)}), bf16[64,8,1280]{2,1,0:T(8,128)(2,1)S(1)}, u32[]{:S(2)}, u32[]{:S(2)}) async-start(bf16[64,8,1280]{2,1,0:T(8,128)(2,1)} %bitcast.9), calls=%async_computation | async-start | bytes 2621440 | tf_op jit(solution)/shard_map/all_to_all | solution.py:270
  22.7 0.0 reduce-scatter.2.cloned.1.call-start
  22.7 24.5 %all-to-all-done = bf16[64,8,1280]{2,1,0:T(8,128)(2,1)S(1)} async-done(((bf16[64,8,1280]{2,1,0:T(8,128)(2,1)}), bf16[64,8,1280]{2,1,0:T(8,128)(2,1)S(1)}, u32[]{:S(2)}, u32[]{:S(2)}) %all-to-all-start) | async-done | bytes 1310752 | tf_op jit(solution)/shard_map/all_to_all | solution.py:270
  47.2 0.0 copy-start
  47.2 52.2 %all-gather.2.cloned.1.call-done = bf16[1,2048,1024]{2,1,0:T(8,128)(2,1)} async-done(((bf16[1,128,1024]{2,1,0:T(8,128)(2,1)}), bf16[1,2048,1024]{2,1,0:T(8,128)(2,1)}) %all-gather.2.cloned.1.call-update) | async-done | bytes 4194320 | tf_op jit(solution)/shard_map/all_gather | solution.py:257
  99.5 0.0 copy-done
  99.5 22.1 %attend.1 = (bf16[512,640]{1,0:T(8,128)(2,1)}, bf16[2048,512]{1,0:T(8,128)(2,1)}) custom-call(s32[1]{0:T(128)} %bitcast.1.side_ref, bf16[512,1280]{1,0:T(8,128)(2,1)} %bitcast.8, bf16[2048,1024]{1,0:T(8,128)(2,1)} %bitcast.14), custom_call_target="tpu_custom_call" | custom-call | flops 6710886400 | bytes 6291456 | tf_op jit(solution)/shard_map/attend/pallas_call | solution.py:272
  121.6 0.0 reduce-scatter.2.cloned.1.call-update
  121.6 7.9 %all-to-all-start.1 = ((bf16[64,8,640]{2,1,0:T(8,128)(2,1)}), bf16[64,8,640]{2,1,0:T(8,128)(2,1)S(1)}, u32[]{:S(2)}, u32[]{:S(2)}) async-start(bf16[64,8,640]{2,1,0:T(8,128)(2,1)} %bitcast.5), calls=%async_computation.1 | async-start | bytes 1310720 | tf_op jit(solution)/shard_map/all_to_all | solution.py:294
  129.5 54.3 %reduce-scatter.2.cloned.1.call-done.own_ref = bf16[256,512]{1,0:T(8,128)(2,1)} async-done(((bf16[2048,512]{1,0:T(8,128)(2,1)}), bf16[256,512]{1,0:T(8,128)(2,1)}) %reduce-scatter.2.cloned.1.call-update) | async-done | bytes 262160 | tf_op jit(solution)/shard_map/reduce_scatter | solution.py:283
  183.8 0.9 slice.4
  184.7 1.9 collective-permute-start
  186.7 0.0 all-to-all-done.1
  186.7 0.0 copy-start.1
  186.7 0.8 copy-done.1
  187.5 2.8 %unpack.1 = bf16[128,2048]{1,0:T(8,128)(2,1)} custom-call(s32[1,128]{1,0:T(1,128)} %bitcast.13, s32[128,1]{1,0:T(8,128)} %copy.7.col_ref, bf16[512,640]{1,0:T(8,128)(2,1)} %bitcast.10), custom_call_target="tpu_custom_call" | custom-call | flops 2147483648 | bytes 3145728 | tf_op jit(solution)/shard_map/unpack/pallas_call | solution.py:295
  190.3 1.3 collective-permute-done.other_ref
  191.6 0.0 copy-start.2
  191.6 0.6 copy-done.2
  192.3 1.8 join.1
Async XLA Ops:
  7.2 92.3 %all-gather.2.cloned.1.call-start = ((), (), s32[]{:S(2)}) async-start(), calls=%async_computation.3 | async-start | bytes 4456448 | tf_op jit(solution)/shard_map/all_gather | solution.py:257
  12.7 34.5 %all-to-all-start = ((bf16[64,8,1280]{2,1,0:T(8,128)(2,1)}), bf16[64,8,1280]{2,1,0:T(8,128)(2,1)S(1)}, u32[]{:S(2)}, u32[]{:S(2)}) async-start(bf16[64,8,1280]{2,1,0:T(8,128)(2,1)} %bitcast.9), calls=%async_computation | async-start | bytes 2621440 | tf_op jit(solution)/shard_map/all_to_all | solution.py:270
  22.7 161.1 %reduce-scatter.2.cloned.1.call-start = ((), (), s32[]{:S(2)}) async-start(), calls=%async_computation.4 | async-start | bytes 2359296 | tf_op jit(solution)/shard_map/reduce_scatter | solution.py:283
  47.2 52.2 %copy-start = (bf16[64,8,1280]{2,1,0:T(8,128)(2,1)}, bf16[64,8,1280]{2,1,0:T(8,128)(2,1)S(1)}, u32[]{:S(2)}) copy-start(bf16[64,8,1280]{2,1,0:T(8,128)(2,1)S(1)} %all-to-all-done) | copy-start | bytes 3932164
  121.6 65.1 %all-to-all-start.1 = ((bf16[64,8,640]{2,1,0:T(8,128)(2,1)}), bf16[64,8,640]{2,1,0:T(8,128)(2,1)S(1)}, u32[]{:S(2)}, u32[]{:S(2)}) async-start(bf16[64,8,640]{2,1,0:T(8,128)(2,1)} %bitcast.5), calls=%async_computation.1 | async-start | bytes 1310720 | tf_op jit(solution)/shard_map/all_to_all | solution.py:294
  184.7 6.9 %collective-permute-start = (bf16[128,512]{1,0:T(8,128)(2,1)S(1)}, bf16[128,512]{1,0:T(8,128)(2,1)S(1)}, u32[]{:S(2)}, u32[]{:S(2)}) collective-permute-start(bf16[128,512]{1,0:T(8,128)(2,1)S(1)} %slice.4), channel_id=1, source_target_pairs={{0,1},{1,0},{2,3},{3,2},{4,5},{5,4},{6,7},{7,6},{8,9},{9,8},{10,11... | collective-permute-start | bytes 393224 | tf_op jit(solution)/shard_map/ppermute | solution.py:284
  186.7 0.8 copy-start.1
  191.6 0.7 copy-start.2
Sparse Core Ops, SparseCore 0:
  10.1 89.3 all-gather.1
  121.7 62.0 reduce-scatter.1
